TPU v7x, 256 devices: a whole 4x4x8 slice. The times are simulated.
256 devices in a mesh: gx: 16 (over x, y), gy: 8 (over z), cores: 2 (over core).
Axes of the slice: x: 4, y: 4, z: 8, core: 2. Of those that a mesh axis runs over, the one named last changes fastest.
Arguments:
- conserved: float32 [5, 512, 512, 128], P(None, 'gx', ('gy', 'cores')), as said below
- box_level: int32 [32, 32], P('gx', ('gy', 'cores')), may hold values from 0 to 1
- box_owner: int32 [32, 32], P('gx', ('gy', 'cores')), may hold values from 0 to 15, as said below
Outputs:
- relocated: float32 [4096, 5, 16, 16, 128], P(('gx', 'gy', 'cores'))
Inputs may be any that keep to these rules, and one draw needn't show every extreme that they name: `box_owner`: among the boxes of one device (an aligned 2 x 2 block of the box grid) no value occurs more than 1 times, and some value occurs exactly 1 times. `conserved`: density and pressure lie in 0.5 to 2 at every cell and each velocity component in -0.8 to 0.8.
All inputs are finite; a program needn't handle non-finite values.
Results may differ from a plain program's by a relative error of at most 0.0003.
Values sent between devices are 32-bit elements; how exact they have to be, the bound alone decides.
No kernel may reach another device: no remote copies, remote signals or barrier semaphores. Data moves between devices by JAX's collectives and lax.ppermute only.
A program may use at most 128 MiB of HBM per device.

v0:
```python
import jax
import jax.numpy as jnp
from jax import lax
from jax.experimental import pallas as pl
from jax.experimental.pallas import tpu as pltpu
from jax.sharding import PartitionSpec as P

BS = 16
NB = 2
SIDE = BS * NB
DEPTH = 128
XE = SIDE + 4
GAMMA = 1.4
STEP = 0.06
HALF = 0.25 * STEP

TILES = 4
HALO = 4
CHUNK = 8


def prims(u):
    r, mx, my, mz, e = u
    inv = pl.reciprocal(r, approx=True)
    inv = inv * (2.0 - r * inv)
    vx, vy, vz = mx * inv, my * inv, mz * inv
    p = (GAMMA - 1.0) * (e - 0.5 * (mx * vx + my * vy + mz * vz))
    a = GAMMA * p * inv
    c = a * lax.rsqrt(a)
    return vx, vy, vz, p, c, e + p


def x_side(u, q):
    vx, _, _, p, c, h = q
    return u, [u[1], u[1] * vx + p, u[2] * vx, u[3] * vx, h * vx], jnp.abs(vx) + c


def y_side(u, q):
    _, vy, _, p, c, h = q
    return u, [u[2], u[1] * vy, u[2] * vy + p, u[3] * vy, h * vy], jnp.abs(vy) + c


def z_side(u, q):
    _, _, vz, p, c, h = q
    return u, [u[3], u[1] * vz, u[2] * vz, u[3] * vz + p, h * vz], jnp.abs(vz) + c


def rusanov(lower, upper):
    ua, fa, sa = lower
    ub, fb, sb = upper
    s = jnp.maximum(sa, sb)
    return [(fa[c] + fb[c]) - s * (ub[c] - ua[c]) for c in range(5)]


def each(side, f, shared):
    u, fl, s = side
    nu = [f(v) for v in u]
    return nu, [nu[shared]] + [f(v) for v in fl[1:]], f(s)


def both(pred, a, b, shared):
    ua, fa, sa = a
    ub, fb, sb = b
    u = [jnp.where(pred, v, w) for v, w in zip(ua, ub)]
    f = [u[shared]] + [jnp.where(pred, v, w) for v, w in zip(fa[1:], fb[1:])]
    return u, f, jnp.where(pred, sa, sb)


def z_faces(side, first, last):
    u, fz, sz = side
    face = rusanov(side, each(side, lambda v: pltpu.roll(v, DEPTH - 1, 1), 3))
    wall = 2.0 * fz[3]
    push = 2.0 * sz * u[3]
    walls = jnp.where(first, wall - push, jnp.where(last, -wall - push, 0.0))
    return [jnp.where(last, 0.0, f) for f in face], walls


def kernel(
    level, owner, cons, xlo, xhi, ylo, yhi, send,
    wn, wg, md, out, zero, fxp, fzp, fxw, fxm, fyw, msk, lvx, in_sem, x_sem, zero_sem, out_sem,
):
    def part(x):
        return pltpu.make_async_copy(
            cons.at[:, pl.ds(x - 2, CHUNK)], wn.at[:, pl.ds(x, CHUNK)], in_sem.at[(x - 2) // CHUNK]
        )

    low = pltpu.make_async_copy(xlo.at[pl.ds(0, 5)], wn.at[:, pl.ds(0, 2)], x_sem.at[0])
    high = pltpu.make_async_copy(xhi.at[pl.ds(0, 5)], wn.at[:, pl.ds(SIDE + 2, 2)], x_sem.at[1])
    low_level = pltpu.make_async_copy(xlo.at[5, 0], lvx.at[0], x_sem.at[2])
    high_level = pltpu.make_async_copy(xhi.at[5, 0], lvx.at[1], x_sem.at[3])
    low.start()
    for i in range(SIDE // CHUNK):
        part(2 + CHUNK * i).start()
    for copy in (high, low_level, high_level):
        copy.start()

    own = [owner[i] for i in range(NB * NB)]
    lev = [[level[NB * a + b].astype(jnp.float32) for b in range(NB)] for a in range(NB)]

    def stage(x, _):
        for c in range(5):
            wg[c, x, 0:1, :] = ylo[c, x, 1:2, :]
            wg[c, x, 1:2, :] = ylo[c, x, 0:1, :]
            wg[c, x, 6:7, :] = yhi[c, x, 1:2, :]
            wg[c, x, 7:8, :] = yhi[c, x, 0:1, :]
        return 0

    lax.fori_loop(0, XE, stage, 0, unroll=2)

    zero[...] = jnp.zeros_like(zero)

    def filled(slot):
        return (own[0] == slot) | (own[1] == slot) | (own[2] == slot) | (own[3] == slot)

    for slot in range(16):
        @pl.when(jnp.logical_not(filled(slot)))
        def _():
            pltpu.make_async_copy(zero, send.at[slot], zero_sem.at[slot]).start()

    lane = lax.broadcasted_iota(jnp.int32, (8, DEPTH), 1)
    sub = lax.broadcasted_iota(jnp.int32, (8, DEPTH), 0)
    first, last = lane == 0, lane == DEPTH - 1
    bottom, top = sub == 0, sub == 7

    for a in range(NB):
        coarse = [1.0 - lev[a][b] for b in range(NB)]
        below = ylo[5, 2 + BS * a, 0:1, :]
        above = yhi[5, 2 + BS * a, 0:1, :]
        msk[a, 0, :, :] = jnp.where(sub < 4, lev[a][0], lev[a][1])
        msk[a, 1, :, :] = jnp.where(
            sub == 3, HALF * coarse[0] * lev[a][1], jnp.where(top, HALF * coarse[1] * above, 0.0)
        )
        msk[a, 2, :, :] = jnp.where(
            sub == 4, HALF * coarse[1] * lev[a][0], jnp.where(bottom, HALF * coarse[0] * below, 0.0)
        )

    def spread(ref, c, x, t):
        return ref[c, x, pl.ds(t, 8, stride=4), :]

    def load_w(x, t):
        if t == HALO:
            return [wg[c, x] for c in range(5)]
        return [spread(wn, c, x, t) for c in range(5)]

    def load_m(x, t):
        return [md[c, x, t] for c in range(5)]

    def keep_x(t, side):
        _, f, s = side
        for c in range(4):
            fxp[c, t] = f[c + 1]
        fxp[4, t] = s

    def x_face(load, x, t, side):
        u = load(x - 1, t)
        return rusanov((u, [u[1]] + [fxp[c, t] for c in range(4)], fxp[4, t]), side)

    def up(v):
        return pltpu.roll(v, 7, 0)

    def down(v):
        return pltpu.roll(v, 1, 0)

    def z_change(t):
        f = [fzp[c, t] for c in range(5)]
        return [v - pltpu.roll(v, 1, 1) for v in f]

    def sweep(load, x, whole):
        cells, faces, ends, change, side = [], [], [], [], []
        for t in range(TILES + 1):
            u = load(x, t)
            q = prims(u)
            side.append(y_side(u, q))
            if t < TILES or whole:
                sx = x_side(u, q)
                face = x_face(load, x, t, sx)
                keep_x(t, sx)
                dz = z_change(t)
                fz, walls = z_faces(z_side(u, q), first, last)
                for c in range(5):
                    fzp[c, t] = fz[c]
                cells.append(u)
                faces.append(face)
                ends.append([face[c] + dz[c] for c in range(5)])
                change.append([face[c] + walls if c == 3 else face[c] for c in range(5)])
            if 0 < t < TILES:
                fy = rusanov(side[t - 1], side[t])
                change[t - 1] = [change[t - 1][c] - fy[c] for c in range(5)]
                change[t] = [change[t][c] + fy[c] for c in range(5)]
        inner = rusanov(side[3], each(side[0], up, 2))
        edge = rusanov(both(top, side[3], side[4], 2), both(top, side[4], side[0], 2))
        after = [jnp.where(top, edge[c], inner[c]) for c in range(5)]
        before = [jnp.where(bottom, edge[c], down(inner[c])) for c in range(5)]
        change[3] = [change[3][c] - after[c] for c in range(5)]
        change[0] = [change[0][c] + before[c] for c in range(5)]
        if whole:
            outer = rusanov(both(top, side[4], each(side[4], up, 2), 2), both(top, each(side[4], down, 2), side[4], 2))
            for c in range(5):
                d = edge[c] - outer[c]
                change[4][c] = change[4][c] + jnp.where(top, d, -d)
        return cells, faces, ends, change, before, after

    def face_slot(x):
        back = x - 2
        return jnp.where(back % BS == 0, back // BS, 3)

    low.wait()
    for t in range(TILES + 1):
        u = load_w(0, t)
        keep_x(t, x_side(u, prims(u)))

    def first_step(x, _):
        @pl.when(((x - 2) % CHUNK == 0) & (x < SIDE + 2))
        def _():
            part(x).wait()

        @pl.when(x == SIDE + 2)
        def _():
            high.wait()

        slot = face_slot(x)
        cells, faces, ends, change, before, after = sweep(load_w, x, True)
        for c in range(5):
            for t in range(TILES + 1):
                md[c, x - 1, t] = md[c, x - 1, t] - HALF * ends[t][c]
                md[c, x, t] = cells[t][c] + HALF * change[t][c]
                if t < TILES:
                    fxw[c, slot, t] = faces[t][c]
            fyw[0, c, x] = before[c]
            fyw[1, c, x] = after[c]
        return 0

    lax.fori_loop(1, XE, first_step, 0)

    for t in range(TILES):
        u = load_m(1, t)
        keep_x(t, x_side(u, prims(u)))

    def second_step(x, _):
        slot = face_slot(x)
        row = jnp.maximum(x - 3, 0)
        fine_back = HALF * msk[row // BS, 0]
        a = (x - 2) // BS
        fine = msk[a, 0]
        coarse = 1.0 - fine
        fine_here = HALF * fine
        at_top, at_bottom = msk[a, 1], msk[a, 2]
        cells, faces, ends, change, before, after = sweep(load_m, x, False)
        for c in range(5):
            for t in range(TILES):
                fxm[c, slot, t] = faces[t][c]
                at = pl.ds(t, 8, stride=4)
                out[c, row, at, :] = out[c, row, at, :] - fine_back * ends[t][c]
                u = cells[t][c]
                v = u + coarse * (u - spread(wn, c, x, t)) + fine_here * change[t][c]
                if t == 0:
                    v = v + at_bottom * (before[c] - fyw[0, c, x])
                if t == 3:
                    v = v - at_top * (after[c] - fyw[1, c, x])
                out[c, x - 2, at, :] = v
        return 0

    def correct(k):
        below = lvx[0, pl.ds(0, 8, stride=4), :] if k == 0 else msk[k - 1, 0]
        above = lvx[1, pl.ds(0, 8, stride=4), :] if k == NB else msk[k, 0]
        to_below = (HALF * (1.0 - below)) * above
        to_above = (HALF * (1.0 - above)) * below
        for t in range(TILES):
            at = pl.ds(t, 8, stride=4)
            for c in range(5):
                d = fxm[c, k, t] - fxw[c, k, t]
                if k > 0:
                    out[c, BS * k - 1, at, :] = out[c, BS * k - 1, at, :] - to_below * d
                if k < NB:
                    out[c, BS * k, at, :] = out[c, BS * k, at, :] + to_above * d

    done = []

    def ship(a):
        for b in range(NB):
            i = NB * a + b
            copy = pltpu.make_async_copy(
                out.at[:, pl.ds(BS * a, BS), pl.ds(BS * b, BS), :], send.at[own[i]], out_sem.at[i]
            )
            copy.start()
            done.append(copy)

    lax.fori_loop(2, BS + 3, second_step, 0)
    low_level.wait()
    high_level.wait()
    correct(0)
    correct(1)
    ship(0)
    lax.fori_loop(BS + 3, SIDE + 2, second_step, 0)
    for t in range(TILES):
        u = load_m(SIDE + 2, t)
        face = x_face(load_m, SIDE + 2, t, x_side(u, prims(u)))
        dz = z_change(t)
        at = pl.ds(t, 8, stride=4)
        for c in range(5):
            fxm[c, 2, t] = face[c]
            out[c, SIDE - 1, at, :] = out[c, SIDE - 1, at, :] - (HALF * msk[NB - 1, 0]) * (face[c] + dz[c])
    correct(2)
    ship(1)
    for copy in done:
        copy.wait()
    for slot in range(16):
        @pl.when(jnp.logical_not(filled(slot)))
        def _():
            pltpu.make_async_copy(zero, send.at[slot], zero_sem.at[slot]).wait()


def update(level, owner, cons, xlo, xhi, ylo, yhi):
    smem = pl.BlockSpec(memory_space=pltpu.SMEM)
    vmem = pl.BlockSpec(memory_space=pltpu.VMEM)
    hbm = pl.BlockSpec(memory_space=pl.ANY)

    def tiles(*lead):
        return pltpu.VMEM(lead + (8, DEPTH), jnp.float32)

    return pl.pallas_call(
        kernel,
        out_shape=jax.ShapeDtypeStruct((16, 5, BS, BS, DEPTH), jnp.float32),
        in_specs=[smem, smem, hbm, hbm, hbm, vmem, vmem],
        out_specs=hbm,
        scratch_shapes=[
            pltpu.VMEM((5, XE, SIDE, DEPTH), jnp.float32),
            tiles(5, XE),
            tiles(5, XE, TILES + 1),
            pltpu.VMEM((5, SIDE, SIDE, DEPTH), jnp.float32),
            pltpu.VMEM((5, BS, BS, DEPTH), jnp.float32),
            tiles(5, TILES + 1),
            tiles(5, TILES + 1),
            tiles(5, 4, TILES),
            tiles(5, 4, TILES),
            tiles(2, 5, XE),
            tiles(NB, 3),
            pltpu.VMEM((2, SIDE, DEPTH), jnp.float32),
            pltpu.SemaphoreType.DMA((SIDE // CHUNK,)),
            pltpu.SemaphoreType.DMA((4,)),
            pltpu.SemaphoreType.DMA((16,)),
            pltpu.SemaphoreType.DMA((4,)),
        ],
        compiler_params=pltpu.CompilerParams(vmem_limit_bytes=51 * 1024 * 1024),
        cost_estimate=pl.CostEstimate(flops=50_000_000, bytes_accessed=14_000_000, transcendentals=600_000),
    )(level, owner, cons, xlo, xhi, ylo, yhi)


def shifted(block, axis, step):
    n = lax.axis_size(axis)
    return lax.ppermute(block, axis, [(i, (i + step) % n) for i in range(n)])


def x_pack(cells, levels):
    plane = jnp.broadcast_to(jnp.repeat(levels, BS)[None, None, :, None], (1, 2, SIDE, DEPTH))
    return jnp.concatenate([cells, plane], axis=0)


def y_pack(cons, xlo, xhi, levels, at):
    cells = jnp.concatenate([xlo[:5, :, at], cons[:, :, at], xhi[:5, :, at]], axis=1)
    plane = jnp.pad(jnp.repeat(levels, BS), (2, 2))
    plane = jnp.broadcast_to(plane[None, :, None, None], (1, XE, 2, DEPTH))
    return jnp.concatenate([cells, plane], axis=0)


def body(conserved, box_level, box_owner):
    rows = ("gy", "cores")
    lev = box_level.astype(jnp.float32)
    xlo = shifted(x_pack(conserved[:, SIDE - 2 :], lev[NB - 1]), "gx", 1)
    xhi = shifted(x_pack(conserved[:, :2], lev[0]), "gx", -1)
    ylo = shifted(y_pack(conserved, xlo, xhi, lev[:, NB - 1], slice(SIDE - 2, SIDE)), rows, 1)
    yhi = shifted(y_pack(conserved, xlo, xhi, lev[:, 0], slice(0, 2)), rows, -1)
    send = update(box_level.reshape(-1), box_owner.reshape(-1), conserved, xlo, xhi, ylo, yhi)
    return lax.all_to_all(send, "gx", split_axis=0, concat_axis=0, tiled=True)


def solution(mesh):
    rows = ("gy", "cores")
    return jax.shard_map(
        body,
        mesh=mesh,
        in_specs=(P(None, "gx", rows, None), P("gx", rows), P("gx", rows)),
        out_specs=P(("gx", "gy", "cores"), None, None, None, None),
        check_vma=False,
    )
```

profile of v0, /device:TPU:6, one launch (start us, length us, event | category | flops | bytes accessed | tf_op | source)
XLA Modules:
  0.0 165.0 jit_solution(18258652814741517192)
XLA Ops:
  0.0 0.7 convert_element_type.6
  0.7 0.1 broadcast_in_dim.38
  0.8 0.1 broadcast_in_dim.39
  0.8 1.0 fusion.1
  1.9 0.1 broadcast_in_dim.40
  2.0 1.7 %collective-permute-start = (f32[6,2,32,128]{3,2,1,0:T(8,128)S(1)}, f32[6,2,32,128]{3,2,1,0:T(8,128)S(1)}, u32[]{:S(2)}, u32[]{:S(2)}) collective-permute-start(f32[6,2,32,128]{3,2,1,0:T(8,128)S(1)} %pad_maximum_fusion.2), channel_id=1, source_target_pairs={{0,16},{16,32},{32,48},{48,64},{64,80},{80,96},{96,112},{112,128},... | collective-permute-start | bytes 589832 | tf_op jit(solution)/shard_map/ppermute | solution.py:351
  3.6 0.1 broadcast_in_dim.41
  3.7 0.1 broadcast_in_dim.42
  3.8 0.1 broadcast_in_dim.43
  3.9 2.6 %collective-permute-start.1 = (f32[6,2,32,128]{3,2,1,0:T(8,128)S(1)}, f32[6,2,32,128]{3,2,1,0:T(8,128)S(1)}, u32[]{:S(2)}, u32[]{:S(2)}) collective-permute-start(f32[6,2,32,128]{3,2,1,0:T(8,128)S(1)} %pad_maximum_fusion.3), channel_id=1, source_target_pairs={{0,240},{16,0},{32,16},{48,32},{64,48},{80,64},{96,80},{112,96},{1... | collective-permute-start | bytes 589832 | tf_op jit(solution)/shard_map/ppermute | solution.py:351
  6.5 0.2 slice_reduce_fusion
  6.7 0.1 broadcast_in_dim.46
  6.7 0.1 reshape.27
  6.8 0.1 broadcast_in_dim.44
  6.9 0.1 reshape.26
  7.0 0.1 pad.8
  7.1 0.1 pad.7
  7.1 1.4 fusion
  8.6 2.2 %collective-permute-done.xlo = f32[6,2,32,128]{3,2,1,0:T(8,128)S(1)} collective-permute-done((f32[6,2,32,128]{3,2,1,0:T(8,128)S(1)}, f32[6,2,32,128]{3,2,1,0:T(8,128)S(1)}, u32[]{:S(2)}, u32[]{:S(2)}) %collective-permute-start) | collective-permute-done | bytes 196640 | tf_op jit(solution)/shard_map/ppermute | solution.py:351
  10.8 0.1 broadcast_in_dim.45
  10.9 0.1 pad_maximum_fusion
  11.0 0.0 collective-permute-start.2
  11.1 0.1 broadcast_in_dim.47
  11.2 0.1 pad_maximum_fusion.1
  11.3 4.4 %collective-permute-start.3 = (f32[6,36,2,128]{3,2,1,0:T(2,128)S(1)}, f32[6,36,2,128]{3,2,1,0:T(2,128)S(1)}, u32[]{:S(2)}, u32[]{:S(2)}) collective-permute-start(f32[6,36,2,128]{3,2,1,0:T(2,128)S(1)} %pad_maximum_fusion.1), channel_id=1, source_target_pairs={{0,15},{1,0},{2,1},{3,2},{4,3},{5,4},{6,5},{7,6},{8,7},{9,8},{10,9... | collective-permute-start | bytes 663560 | tf_op jit(solution)/shard_map/ppermute | solution.py:351
  15.7 0.8 reshape.24.level
  16.5 0.8 reshape.25.owner
  17.2 1.9 %collective-permute-done.2.ylo = f32[6,36,2,128]{3,2,1,0:T(2,128)S(1)} collective-permute-done((f32[6,36,2,128]{3,2,1,0:T(2,128)S(1)}, f32[6,36,2,128]{3,2,1,0:T(2,128)S(1)}, u32[]{:S(2)}, u32[]{:S(2)}) %collective-permute-start.2) | collective-permute-done | bytes 221216 | tf_op jit(solution)/shard_map/ppermute | solution.py:351
  19.1 0.1 collective-permute-done.3.yhi
  19.2 15.5 %shard_map.37 = f32[16,5,16,16,128]{4,3,2,1,0:T(8,128)} custom-call(s32[4]{0:T(128)S(1)} %reshape.24.level, s32[4]{0:T(128)S(1)} %reshape.25.owner, f32[5,32,32,128]{3,2,1,0:T(8,128)} %cons.1, f32[6,2,32,128]{3,2,1,0:T(8,128)S(1)} %collective-permute-done.xlo, f32[6,2,32,128]{3,2,1,0:T(8,128)S(1)} %collective-permute-done.1.xhi, ...), custom_call_target="tpu_custom_call" | custom-call | flops 50000000 | bytes 14000000 | tf_op jit(solution)/shard_map/pallas_call | solution.py:321
  34.7 126.3 %all_to_all.5 = f32[16,5,16,16,128]{4,3,2,1,0:T(8,128)S(1)} all-to-all(f32[16,5,16,16,128]{4,3,2,1,0:T(8,128)} %shard_map.37), channel_id=1, replica_groups=mesh['gx'=16,'gy'=8,'cores'=2] {'gx'}, dimensions={0} | all-to-all | bytes 20971520 | tf_op jit(solution)/shard_map/all_to_all | solution.py:374
  161.0 4.1 %copy.5 = f32[16,5,16,16,128]{4,3,2,1,0:T(8,128)} copy(f32[16,5,16,16,128]{4,3,2,1,0:T(8,128)S(1)} %all_to_all.5) | data formatting | bytes 20971520
  (6 shorter events, 0.1 us)
Async XLA Ops:
  2.0 8.8 %collective-permute-start = (f32[6,2,32,128]{3,2,1,0:T(8,128)S(1)}, f32[6,2,32,128]{3,2,1,0:T(8,128)S(1)}, u32[]{:S(2)}, u32[]{:S(2)}) collective-permute-start(f32[6,2,32,128]{3,2,1,0:T(8,128)S(1)} %pad_maximum_fusion.2), channel_id=1, source_target_pairs={{0,16},{16,32},{32,48},{48,64},{64,80},{80,96},{96,112},{112,128},... | collective-permute-start | bytes 589832 | tf_op jit(solution)/shard_map/ppermute | solution.py:351
  3.9 6.9 %collective-permute-start.1 = (f32[6,2,32,128]{3,2,1,0:T(8,128)S(1)}, f32[6,2,32,128]{3,2,1,0:T(8,128)S(1)}, u32[]{:S(2)}, u32[]{:S(2)}) collective-permute-start(f32[6,2,32,128]{3,2,1,0:T(8,128)S(1)} %pad_maximum_fusion.3), channel_id=1, source_target_pairs={{0,240},{16,0},{32,16},{48,32},{64,48},{80,64},{96,80},{112,96},{1... | collective-permute-start | bytes 589832 | tf_op jit(solution)/shard_map/ppermute | solution.py:351
  11.0 8.1 %collective-permute-start.2 = (f32[6,36,2,128]{3,2,1,0:T(2,128)S(1)}, f32[6,36,2,128]{3,2,1,0:T(2,128)S(1)}, u32[]{:S(2)}, u32[]{:S(2)}) collective-permute-start(f32[6,36,2,128]{3,2,1,0:T(2,128)S(1)} %pad_maximum_fusion), channel_id=1, source_target_pairs={{0,1},{1,2},{2,3},{3,4},{4,5},{5,6},{6,7},{7,8},{8,9},{9,10},{10,1... | collective-permute-start | bytes 663560 | tf_op jit(solution)/shard_map/ppermute | solution.py:351
  11.3 7.9 %collective-permute-start.3 = (f32[6,36,2,128]{3,2,1,0:T(2,128)S(1)}, f32[6,36,2,128]{3,2,1,0:T(2,128)S(1)}, u32[]{:S(2)}, u32[]{:S(2)}) collective-permute-start(f32[6,36,2,128]{3,2,1,0:T(2,128)S(1)} %pad_maximum_fusion.1), channel_id=1, source_target_pairs={{0,15},{1,0},{2,1},{3,2},{4,3},{5,4},{6,5},{7,6},{8,7},{9,8},{10,9... | collective-permute-start | bytes 663560 | tf_op jit(solution)/shard_map/ppermute | solution.py:351
where the time goes:
time: 165 us
  blocking collectives  126 us (76%)
  Pallas kernels  15.5 us (9%)
  local copies, waits for them, and re-layouts  9.33 us (6%)
  starting transfers between devices  8.74 us (5%)
  waiting for transfers between devices  4.17 us (3%)
    all_to_all x1, blocking collectives, body(): return lax.all_to_all(send, 'gx', split_axis=0, concat_axis=0, tiled=True)  126 us
    pallas_call x1, Pallas kernels, update(): pl.pallas_call(kernel, out_shape=jax.ShapeDtypeStruct((16, 5, BS, BS, DEP...  15.5 us
    ppermute x4, starting transfers between devices, shifted(): return lax.ppermute(block, axis, [(i, (i + step) % n) for i in range(n)])  8.74 us
    ppermute x4, waiting for transfers between devices, shifted(): return lax.ppermute(block, axis, [(i, (i + step) % n) for i in range(n)])  4.17 us
    unnamed x1, local copies, waits for them, and re-layouts  4.09 us
  transfers between devices with their start and end apart: 4, of which 3 were waited for; matrix products, arithmetic and copies ran while one was open for 2% of the time, Pallas kernels for 0%

commit v1 on v0

--- a/solution.py
+++ b/solution.py
@@ -1,3 +1,5 @@
+import functools
+
 import jax
 import jax.numpy as jnp
 from jax import lax
@@ -17,6 +19,10 @@
 TILES = 4
 HALO = 4
 CHUNK = 8
+
+QX = BS // 4
+PACKET = (5, QX, BS, DEPTH)
+OWN = (21, QX, BS, DEPTH)
 
 
 def prims(u):
@@ -76,8 +82,8 @@
 
 
 def kernel(
-    level, owner, cons, xlo, xhi, ylo, yhi, send,
-    wn, wg, md, out, zero, fxp, fzp, fxw, fxm, fyw, msk, lvx, in_sem, x_sem, zero_sem, out_sem,
+    level, owner, cons, xlo, xhi, ylo_in, yhi_in, own0, own1, own2, own3,
+    wn, wg, md, out, note, fxp, fzp, fxw, fxm, fyw, msk, lvx, ylo, yhi, in_sem, x_sem, y_sem, out_sem, note_sem,
 ):
     def part(x):
         return pltpu.make_async_copy(
@@ -88,14 +94,19 @@
     high = pltpu.make_async_copy(xhi.at[pl.ds(0, 5)], wn.at[:, pl.ds(SIDE + 2, 2)], x_sem.at[1])
     low_level = pltpu.make_async_copy(xlo.at[5, 0], lvx.at[0], x_sem.at[2])
     high_level = pltpu.make_async_copy(xhi.at[5, 0], lvx.at[1], x_sem.at[3])
+    y_copies = [pltpu.make_async_copy(ylo_in, ylo, y_sem.at[0]), pltpu.make_async_copy(yhi_in, yhi, y_sem.at[1])]
+    for copy in y_copies:
+        copy.start()
     low.start()
     for i in range(SIDE // CHUNK):
         part(2 + CHUNK * i).start()
     for copy in (high, low_level, high_level):
         copy.start()
 
-    own = [owner[i] for i in range(NB * NB)]
     lev = [[level[NB * a + b].astype(jnp.float32) for b in range(NB)] for a in range(NB)]
+
+    for copy in y_copies:
+        copy.wait()
 
     def stage(x, _):
         for c in range(5):
@@ -106,16 +117,6 @@
         return 0
 
     lax.fori_loop(0, XE, stage, 0, unroll=2)
-
-    zero[...] = jnp.zeros_like(zero)
-
-    def filled(slot):
-        return (own[0] == slot) | (own[1] == slot) | (own[2] == slot) | (own[3] == slot)
-
-    for slot in range(16):
-        @pl.when(jnp.logical_not(filled(slot)))
-        def _():
-            pltpu.make_async_copy(zero, send.at[slot], zero_sem.at[slot]).start()
 
     lane = lax.broadcasted_iota(jnp.int32, (8, DEPTH), 1)
     sub = lax.broadcasted_iota(jnp.int32, (8, DEPTH), 0)
@@ -275,15 +276,22 @@
                     out[c, BS * k, at, :] = out[c, BS * k, at, :] + to_above * d
 
     done = []
+    for i in range(NB * NB):
+        note[i] = jnp.full((BS, DEPTH), corner(owner[i]).astype(jnp.float32))
+    for q, own in enumerate((own0, own1, own2, own3)):
+        copy = pltpu.make_async_copy(note, own.at[20], note_sem.at[q])
+        copy.start()
+        done.append(copy)
 
     def ship(a):
         for b in range(NB):
-            i = NB * a + b
-            copy = pltpu.make_async_copy(
-                out.at[:, pl.ds(BS * a, BS), pl.ds(BS * b, BS), :], send.at[own[i]], out_sem.at[i]
-            )
-            copy.start()
-            done.append(copy)
+            for q, own in enumerate((own0, own1, own2, own3)):
+                i = NB * a + b
+                copy = pltpu.make_async_copy(
+                    out.at[:, pl.ds(BS * a + QX * q, QX), pl.ds(BS * b, BS), :], own.at[pl.ds(5 * i, 5)], out_sem.at[i, q]
+                )
+                copy.start()
+                done.append(copy)
 
     lax.fori_loop(2, BS + 3, second_step, 0)
     low_level.wait()
@@ -304,15 +312,10 @@
     ship(1)
     for copy in done:
         copy.wait()
-    for slot in range(16):
-        @pl.when(jnp.logical_not(filled(slot)))
-        def _():
-            pltpu.make_async_copy(zero, send.at[slot], zero_sem.at[slot]).wait()
 
 
 def update(level, owner, cons, xlo, xhi, ylo, yhi):
     smem = pl.BlockSpec(memory_space=pltpu.SMEM)
-    vmem = pl.BlockSpec(memory_space=pltpu.VMEM)
     hbm = pl.BlockSpec(memory_space=pl.ANY)
 
     def tiles(*lead):
@@ -320,15 +323,15 @@
 
     return pl.pallas_call(
         kernel,
-        out_shape=jax.ShapeDtypeStruct((16, 5, BS, BS, DEPTH), jnp.float32),
-        in_specs=[smem, smem, hbm, hbm, hbm, vmem, vmem],
-        out_specs=hbm,
+        out_shape=[jax.ShapeDtypeStruct(OWN, jnp.float32)] * 4,
+        in_specs=[smem, smem, hbm, hbm, hbm, hbm, hbm],
+        out_specs=[hbm] * 4,
         scratch_shapes=[
             pltpu.VMEM((5, XE, SIDE, DEPTH), jnp.float32),
             tiles(5, XE),
             tiles(5, XE, TILES + 1),
             pltpu.VMEM((5, SIDE, SIDE, DEPTH), jnp.float32),
-            pltpu.VMEM((5, BS, BS, DEPTH), jnp.float32),
+            pltpu.VMEM((QX, BS, DEPTH), jnp.float32),
             tiles(5, TILES + 1),
             tiles(5, TILES + 1),
             tiles(5, 4, TILES),
@@ -336,14 +339,169 @@
             tiles(2, 5, XE),
             tiles(NB, 3),
             pltpu.VMEM((2, SIDE, DEPTH), jnp.float32),
+            pltpu.VMEM((6, XE, 2, DEPTH), jnp.float32),
+            pltpu.VMEM((6, XE, 2, DEPTH), jnp.float32),
             pltpu.SemaphoreType.DMA((SIDE // CHUNK,)),
             pltpu.SemaphoreType.DMA((4,)),
-            pltpu.SemaphoreType.DMA((16,)),
+            pltpu.SemaphoreType.DMA((2,)),
+            pltpu.SemaphoreType.DMA((4, 4)),
             pltpu.SemaphoreType.DMA((4,)),
         ],
-        compiler_params=pltpu.CompilerParams(vmem_limit_bytes=51 * 1024 * 1024),
+        compiler_params=pltpu.CompilerParams(vmem_limit_bytes=60 * 1024 * 1024),
         cost_estimate=pl.CostEstimate(flops=50_000_000, bytes_accessed=14_000_000, transcendentals=600_000),
     )(level, owner, cons, xlo, xhi, ylo, yhi)
+
+
+def corner(g):
+    return g ^ ((g >> 1) & 5)
+
+
+def bit(q, t):
+    return 1 << ((q + t) % 4)
+
+
+def across(block, q, t):
+    return lax.ppermute(block, "gx", [(g, corner(corner(g) ^ bit(q, t))) for g in range(16)])
+
+
+def place(out, me, mask, q):
+    return out.at[corner(me ^ mask), :, pl.ds(QX * q, QX)]
+
+
+def gather(src, me, patterns, stores):
+    notes = [src[20, i, 0:8, :] for i in range(4)]
+    picks = [[note == (me ^ pattern).astype(jnp.float32) for note in notes] for pattern in patterns]
+
+    def body(c, _):
+        for x in range(QX):
+            for part in (slice(0, 8), slice(8, 16)):
+                cells = [src[5 * i + c, x, part, :] for i in range(4)]
+                for pick, store in zip(picks, stores):
+                    v = jnp.zeros((8, DEPTH), jnp.float32)
+                    for i in range(4):
+                        v = jnp.where(pick[i], cells[i], v)
+                    store[c, x, part, :] = v
+        return 0
+
+    lax.fori_loop(0, 5, body, 0)
+
+
+def two_kernel(meta, *refs):
+    low, high, m2 = refs[0:4], refs[4:8], refs[8:12]
+    me = meta[0]
+    for q in range(4):
+        for f0, src in enumerate((low[q], high[q])):
+            patterns = [bit(q, 2) | (b3 * bit(q, 3)) for b3 in range(2)]
+            gather(src, me, patterns, [m2[q].at[2 * f0 + b3] for b3 in range(2)])
+
+
+def four_kernel(meta, *refs):
+    arrays, m3 = refs[0:16], refs[16:20]
+    for q in range(4):
+        for f in range(4):
+            gather(arrays[4 * f + q], meta[0], [bit(q, 3)], [m3[q].at[f]])
+
+
+def end_kernel(meta, *refs):
+    arrays, out, buf, sem = refs[0:16], refs[16], refs[17], refs[18]
+    me = meta[0]
+    copies = []
+    for q in range(4):
+        for f in range(4):
+            f1, f0 = f // 2, f % 2
+            gather(arrays[4 * f + q], me, [0], [buf.at[4 * q + f]])
+            to = place(out, me, f0 * bit(q, 0) | f1 * bit(q, 1), q)
+            copies.append(pltpu.make_async_copy(buf.at[4 * q + f], to, sem.at[4 * q + f]))
+            copies[-1].start()
+    for copy in copies:
+        copy.wait()
+
+
+def pass_kernel(meta, *refs):
+    r2a, r2b, m3b = refs[0:4], refs[4:8], refs[8:12]
+
+    def body(c, _):
+        for q in range(4):
+            for f in range(4):
+                m3b[q][f, c] = (r2a, r2b)[f // 2][q][2 * (f % 2) + 1, c]
+        return 0
+
+    lax.fori_loop(0, 5, body, 0)
+
+
+def place_kernel(kind, flows, meta, *refs):
+    n = len(refs) - 3
+    arrays, out, sem = refs[:n], refs[-2], refs[-1]
+    me = meta[0]
+    copies = []
+    for i, q in enumerate(flows):
+        for f in range(4):
+            f1, f0 = f // 2, f % 2
+            mask = f0 * bit(q, 0) | f1 * bit(q, 1)
+            if kind == 2:
+                src, mask = arrays[len(flows) * f1 + i].at[2 * f0], mask | bit(q, 2)
+            else:
+                src, mask = arrays[i].at[f], mask | ((kind - 3) * bit(q, 2)) | bit(q, 3)
+            copies.append(pltpu.make_async_copy(src, place(out, me, mask, q), sem.at[4 * i + f]))
+    for copy in copies:
+        copy.start()
+    for copy in copies:
+        copy.wait()
+
+
+MOVED = jax.ShapeDtypeStruct((4,) + PACKET, jnp.float32)
+RESULT = jax.ShapeDtypeStruct((16, 5, BS, BS, DEPTH), jnp.float32)
+
+
+def mover(f, outs, meta, *args):
+    hbm = pl.BlockSpec(memory_space=pl.ANY)
+    vmem = pl.BlockSpec(memory_space=pltpu.VMEM)
+    end = outs[0] is RESULT
+    return pl.pallas_call(
+        f,
+        out_shape=outs,
+        in_specs=[pl.BlockSpec(memory_space=pltpu.SMEM)] + [vmem] * len(args),
+        out_specs=[hbm if end else vmem] * len(outs),
+        scratch_shapes=[pltpu.VMEM((16,) + PACKET, jnp.float32), pltpu.SemaphoreType.DMA((16,))] if end else [],
+        compiler_params=pltpu.CompilerParams(vmem_limit_bytes=18 * 1024 * 1024),
+        cost_estimate=pl.CostEstimate(flops=0, bytes_accessed=8_000_000, transcendentals=0),
+    )(meta, *args)
+
+
+def placer(kind, flows, meta, arrays, out):
+    vmem = pl.BlockSpec(memory_space=pltpu.VMEM)
+    hbm = pl.BlockSpec(memory_space=pl.ANY)
+    return pl.pallas_call(
+        functools.partial(place_kernel, kind, flows),
+        out_shape=RESULT,
+        in_specs=[pl.BlockSpec(memory_space=pltpu.SMEM)] + [vmem] * len(arrays) + [hbm],
+        out_specs=hbm,
+        scratch_shapes=[pltpu.SemaphoreType.DMA((4 * len(flows),))],
+        input_output_aliases={1 + len(arrays): 0},
+        compiler_params=pltpu.CompilerParams(vmem_limit_bytes=8 * 1024 * 1024),
+        cost_estimate=pl.CostEstimate(flops=0, bytes_accessed=4_000_000, transcendentals=0),
+    )(meta, *arrays, out)
+
+
+def relocate(own):
+    meta = corner(lax.axis_index("gx")).astype(jnp.int32)[None]
+    flows = range(4)
+    r0 = [across(own[q], q, 0) for q in flows]
+    r1a = [across(own[q], q, 1) for q in flows]
+    r1b = [across(r0[q], q, 1) for q in flows]
+    m2a = mover(two_kernel, [MOVED] * 4, meta, *own, *r0)
+    r2a = [across(m2a[q], q, 2) for q in flows]
+    m2b = mover(two_kernel, [MOVED] * 4, meta, *r1a, *r1b)
+    r2b = [across(m2b[q], q, 2) for q in flows]
+    m3a = mover(four_kernel, [MOVED] * 4, meta, *own, *r0, *r1a, *r1b)
+    r3a = [across(m3a[q], q, 3) for q in flows]
+    m3b = mover(pass_kernel, [MOVED] * 4, meta, *r2a, *r2b)
+    r3b = [across(m3b[q], q, 3) for q in flows]
+    (out,) = mover(end_kernel, [RESULT], meta, *own, *r0, *r1a, *r1b)
+    out = placer(2, (0, 1, 2, 3), meta, r2a + r2b, out)
+    out = placer(3, (0, 1, 2, 3), meta, r3a, out)
+    out = placer(4, (0, 1), meta, r3b[:2], out)
+    return placer(4, (2, 3), meta, r3b[2:], out)
 
 
 def shifted(block, axis, step):
@@ -370,8 +528,9 @@
     xhi = shifted(x_pack(conserved[:, :2], lev[0]), "gx", -1)
     ylo = shifted(y_pack(conserved, xlo, xhi, lev[:, NB - 1], slice(SIDE - 2, SIDE)), rows, 1)
     yhi = shifted(y_pack(conserved, xlo, xhi, lev[:, 0], slice(0, 2)), rows, -1)
-    send = update(box_level.reshape(-1), box_owner.reshape(-1), conserved, xlo, xhi, ylo, yhi)
-    return lax.all_to_all(send, "gx", split_axis=0, concat_axis=0, tiled=True)
+    owner = box_owner.reshape(-1)
+    own = update(box_level.reshape(-1), owner, conserved, xlo, xhi, ylo, yhi)
+    return relocate(own)
 
 
 def solution(mesh):

time: 165 us -> 157 us (0.952); the launches traced: 165 us -> 155 us
  blocking collectives: 126 us -> 0 us
  waiting for transfers between devices: 4.17 us -> 72.7 us
  starting transfers between devices: 8.74 us -> 34.4 us
  Pallas kernels: 15.5 us -> 34.1 us
  local copies, waits for them, and re-layouts: 9.33 us -> 12.1 us
    all_to_all x1 -> x0, blocking collectives: 126 us -> none  [body(): return lax.all_to_all(send, 'gx', split_axis=0, concat_axis=0, tiled=True)]
    ppermute x0 -> x28, waiting for transfers between devices: none -> 69.7 us  [across(): lax.ppermute(block, 'gx', [(g, corner(corner(g) ^ bit(q, t))) for g in ra...]
    ppermute x0 -> x28, starting transfers between devices: none -> 25.6 us  [across(): lax.ppermute(block, 'gx', [(g, corner(corner(g) ^ bit(q, t))) for g in ra...]
    pallas_call x1 -> x10, Pallas kernels: 15.5 us -> 34.1 us  [the longest x1 17 us: update(): pl.pallas_call(kernel, out_shape=[jax.ShapeDtypeStruct(OWN, jnp.float32)]...]
    unnamed x1 -> x24, local copies, waits for them, and re-layouts: 4.09 us -> 5.72 us
  transfers between devices with their start and end apart: 4 -> 32, of which waited for: 3 -> 13; matrix products, arithmetic and copies ran while one was open for 2% -> 3% of each run, Pallas kernels for 0% -> 10%
where the time goes in v1:
time: 157 us; the launch traced here: 155 us
  waiting for transfers between devices  72.7 us (46%)
  starting transfers between devices  34.4 us (22%)
  Pallas kernels  34.1 us (22%)
  local copies, waits for them, and re-layouts  12.1 us (8%)
    ppermute x28, waiting for transfers between devices, across(): lax.ppermute(block, 'gx', [(g, corner(corner(g) ^ bit(q, t))) for g in ra...  69.7 us
    ppermute x28, starting transfers between devices, across(): lax.ppermute(block, 'gx', [(g, corner(corner(g) ^ bit(q, t))) for g in ra...  25.6 us
    pallas_call x1, Pallas kernels, update(): pl.pallas_call(kernel, out_shape=[jax.ShapeDtypeStruct(OWN, jnp.float32)]...  17 us
    pallas_call x5, Pallas kernels, mover(): pl.pallas_call(f, out_shape=outs, in_specs=[pl.BlockSpec(memory_space=plt...  11.6 us
    ppermute x4, starting transfers between devices, shifted(): return lax.ppermute(block, axis, [(i, (i + step) % n) for i in range(n)])  8.74 us
    unnamed x24, local copies, waits for them, and re-layouts  5.72 us
    pallas_call x4, Pallas kernels, placer(): pl.pallas_call(functools.partial(place_kernel, kind, flows), out_shape=RE...  5.48 us
  transfers between devices with their start and end apart: 32, of which 13 were waited for; matrix products, arithmetic and copies ran while one was open for 3% of the time, Pallas kernels for 10%

profile of v1, /device:TPU:6, one launch (start us, length us, event | category | flops | bytes accessed | tf_op | source)
XLA Modules:
  0.0 154.6 jit_solution(13676158398397745595)
XLA Ops:
  2.0 1.7 %collective-permute-start = (f32[6,2,32,128]{3,2,1,0:T(8,128)S(1)}, f32[6,2,32,128]{3,2,1,0:T(8,128)S(1)}, u32[]{:S(2)}, u32[]{:S(2)}) collective-permute-start(f32[6,2,32,128]{3,2,1,0:T(8,128)S(1)} %pad_maximum_fusion.2), channel_id=1, source_target_pairs={{0,16},{16,32},{32,48},{48,64},{64,80},{80,96},{96,112},{112,128},... | collective-permute-start | bytes 589832 | tf_op jit(solution)/shard_map/ppermute | solution.py:509
  3.9 2.6 %collective-permute-start.1 = (f32[6,2,32,128]{3,2,1,0:T(8,128)S(1)}, f32[6,2,32,128]{3,2,1,0:T(8,128)S(1)}, u32[]{:S(2)}, u32[]{:S(2)}) collective-permute-start(f32[6,2,32,128]{3,2,1,0:T(8,128)S(1)} %pad_maximum_fusion.3), channel_id=1, source_target_pairs={{0,240},{16,0},{32,16},{48,32},{64,48},{80,64},{96,80},{112,96},{1... | collective-permute-start | bytes 589832 | tf_op jit(solution)/shard_map/ppermute | solution.py:509
  7.1 1.4 fusion
  8.6 2.2 %collective-permute-done.xlo = f32[6,2,32,128]{3,2,1,0:T(8,128)S(1)} collective-permute-done((f32[6,2,32,128]{3,2,1,0:T(8,128)S(1)}, f32[6,2,32,128]{3,2,1,0:T(8,128)S(1)}, u32[]{:S(2)}, u32[]{:S(2)}) %collective-permute-start) | collective-permute-done | bytes 196640 | tf_op jit(solution)/shard_map/ppermute | solution.py:509
  11.3 4.4 %collective-permute-start.3 = (f32[6,36,2,128]{3,2,1,0:T(2,128)S(1)}, f32[6,36,2,128]{3,2,1,0:T(2,128)S(1)}, u32[]{:S(2)}, u32[]{:S(2)}) collective-permute-start(f32[6,36,2,128]{3,2,1,0:T(2,128)S(1)} %pad_maximum_fusion.1), channel_id=1, source_target_pairs={{0,15},{1,0},{2,1},{3,2},{4,3},{5,4},{6,5},{7,6},{8,7},{9,8},{10,9... | collective-permute-start | bytes 663560 | tf_op jit(solution)/shard_map/ppermute | solution.py:509
  15.7 1.3 reshape.24.level
  17.1 1.3 reshape.25.owner
  20.5 17.0 %shard_map.37 = (f32[21,4,16,128]{3,2,1,0:T(8,128)}, f32[21,4,16,128]{3,2,1,0:T(8,128)}, f32[21,4,16,128]{3,2,1,0:T(8,128)}, f32[21,4,16,128]{3,2,1,0:T(8,128)}) custom-call(s32[4]{0:T(128)} %reshape.24.level, s32[4]{0:T(128)} %reshape.25.owner, f32[5,32,32,128]{3,2,1,0:T(8,128)} %cons.1, f32[6,2,32,128]{3,2,1,0:T(8,128)} %copy-done.8, ...), custom_call_target="tpu_custom_call" | custom-call | flops 50000000 | bytes 14000000 | tf_op jit(solution)/shard_map/pallas_call | solution.py:324
  37.5 4.5 %collective-permute-start.12 = (f32[21,4,16,128]{3,2,1,0:T(8,128)}, f32[21,4,16,128]{3,2,1,0:T(8,128)S(1)}, u32[]{:S(2)}, u32[]{:S(2)}) collective-permute-start(f32[21,4,16,128]{3,2,1,0:T(8,128)} %get-tuple-element.25.refs_0_), channel_id=1, source_target_pairs={{0,48},{16,32},{32,16},{48,0},{64,112},{80,96},{96,80},{112,64},{1... | collective-permute-start | bytes 2064392 | tf_op jit(solution)/shard_map/ppermute | solution.py:364
  42.3 1.3 collective-permute-start.14
  43.7 14.9 %collective-permute-done.12.refs_0_.refs_8_ = f32[21,4,16,128]{3,2,1,0:T(8,128)S(1)} collective-permute-done((f32[21,4,16,128]{3,2,1,0:T(8,128)}, f32[21,4,16,128]{3,2,1,0:T(8,128)S(1)}, u32[]{:S(2)}, u32[]{:S(2)}) %collective-permute-start.12) | collective-permute-done | bytes 688160 | tf_op jit(solution)/shard_map/ppermute | solution.py:364
  58.6 1.4 collective-permute-start.7
  60.0 2.6 %collective-permute-start.15 = (f32[21,4,16,128]{3,2,1,0:T(8,128)}, f32[21,4,16,128]{3,2,1,0:T(8,128)}, u32[]{:S(2)}, u32[]{:S(2)}) collective-permute-start(f32[21,4,16,128]{3,2,1,0:T(8,128)} %get-tuple-element.28.refs_3_), channel_id=1, source_target_pairs={{0,16},{16,0},{32,48},{48,32},{64,80},{80,64},{96,112},{112,96},{1... | collective-permute-start | bytes 2064392 | tf_op jit(solution)/shard_map/ppermute | solution.py:364
  62.6 9.3 %collective-permute-done.5.refs_5_ = f32[21,4,16,128]{3,2,1,0:T(8,128)S(1)} collective-permute-done((f32[21,4,16,128]{3,2,1,0:T(8,128)}, f32[21,4,16,128]{3,2,1,0:T(8,128)S(1)}, u32[]{:S(2)}, u32[]{:S(2)}) %collective-permute-start.5) | collective-permute-done | bytes 688160 | tf_op jit(solution)/shard_map/ppermute | solution.py:364
  71.9 3.0 %collective-permute-start.16 = (f32[21,4,16,128]{3,2,1,0:T(8,128)S(1)}, f32[21,4,16,128]{3,2,1,0:T(8,128)}, u32[]{:S(2)}, u32[]{:S(2)}) collective-permute-start(f32[21,4,16,128]{3,2,1,0:T(8,128)S(1)} %collective-permute-done.4.refs_4_), channel_id=1, source_target_pairs={{0,48},{16,32},{32,16},{48,0},{64,112},{80,96},{96,80},{112,64},{1... | collective-permute-start | bytes 2064392 | tf_op jit(solution)/shard_map/ppermute | solution.py:364
  75.0 1.4 collective-permute-start.18
  81.9 1.9 %shard_map.38 = (f32[4,5,4,16,128]{4,3,2,1,0:T(8,128)S(1)}, f32[4,5,4,16,128]{4,3,2,1,0:T(8,128)S(1)}, f32[4,5,4,16,128]{4,3,2,1,0:T(8,128)S(1)}, f32[4,5,4,16,128]{4,3,2,1,0:T(8,128)S(1)}) custom-call(s32[1]{0:T(128)} %bitcast.meta, f32[21,4,16,128]{3,2,1,0:T(8,128)S(1)} %copy-done, f32[21,4,16,128]{3,2,1,0:T(8,128)S(1)} %copy-done.2, ...), custom_call_target="tpu_custom_call" | custom-call | bytes 8000000 | tf_op jit(solution)/shard_map/pallas_call | solution.py:460
  84.7 4.6 %collective-permute-done.16.refs_4_.refs_12_ = f32[21,4,16,128]{3,2,1,0:T(8,128)} collective-permute-done((f32[21,4,16,128]{3,2,1,0:T(8,128)S(1)}, f32[21,4,16,128]{3,2,1,0:T(8,128)}, u32[]{:S(2)}, u32[]{:S(2)}) %collective-permute-start.16) | collective-permute-done | bytes 688160 | tf_op jit(solution)/shard_map/ppermute | solution.py:364
  89.4 4.0 %collective-permute-done.17.refs_5_.refs_13_ = f32[21,4,16,128]{3,2,1,0:T(8,128)} collective-permute-done((f32[21,4,16,128]{3,2,1,0:T(8,128)S(1)}, f32[21,4,16,128]{3,2,1,0:T(8,128)}, u32[]{:S(2)}, u32[]{:S(2)}) %collective-permute-start.17) | collective-permute-done | bytes 688160 | tf_op jit(solution)/shard_map/ppermute | solution.py:364
  93.6 2.4 %shard_map.39 = (f32[4,5,4,16,128]{4,3,2,1,0:T(8,128)S(1)}, f32[4,5,4,16,128]{4,3,2,1,0:T(8,128)S(1)}, f32[4,5,4,16,128]{4,3,2,1,0:T(8,128)S(1)}, f32[4,5,4,16,128]{4,3,2,1,0:T(8,128)S(1)}) custom-call(s32[1]{0:T(128)} %bitcast.meta, f32[21,4,16,128]{3,2,1,0:T(8,128)S(1)} %collective-permute-done.12.refs_0_.refs_8_, ...), custom_call_target="tpu_custom_call" | custom-call | bytes 8000000 | tf_op jit(solution)/shard_map/pallas_call | solution.py:460
  97.3 10.0 %collective-permute-done.8.refs_0_ = f32[4,5,4,16,128]{4,3,2,1,0:T(8,128)S(1)} collective-permute-done((f32[4,5,4,16,128]{4,3,2,1,0:T(8,128)S(1)}, f32[4,5,4,16,128]{4,3,2,1,0:T(8,128)S(1)}, u32[]{:S(2)}, u32[]{:S(2)}) %collective-permute-start.8) | collective-permute-done | bytes 655392 | tf_op jit(solution)/shard_map/ppermute | solution.py:364
  108.4 3.1 %shard_map.41 = (f32[4,5,4,16,128]{4,3,2,1,0:T(8,128)S(1)}, f32[4,5,4,16,128]{4,3,2,1,0:T(8,128)S(1)}, f32[4,5,4,16,128]{4,3,2,1,0:T(8,128)S(1)}, f32[4,5,4,16,128]{4,3,2,1,0:T(8,128)S(1)}) custom-call(s32[1]{0:T(128)} %bitcast.meta, f32[21,4,16,128]{3,2,1,0:T(8,128)S(1)} %copy-done.1, f32[21,4,16,128]{3,2,1,0:T(8,128)S(1)} %copy-done.3, ...), custom_call_target="tpu_custom_call" | custom-call | bytes 8000000 | tf_op jit(solution)/shard_map/pallas_call | solution.py:460
  111.6 2.5 %collective-permute-start.28 = (f32[4,5,4,16,128]{4,3,2,1,0:T(8,128)S(1)}, f32[4,5,4,16,128]{4,3,2,1,0:T(8,128)S(1)}, u32[]{:S(2)}, u32[]{:S(2)}) collective-permute-start(f32[4,5,4,16,128]{4,3,2,1,0:T(8,128)S(1)} %get-tuple-element.41), channel_id=1, source_target_pairs={{0,192},{16,208},{32,224},{48,240},{64,128},{80,144},{96,160},{112... | collective-permute-start | bytes 1966088 | tf_op jit(solution)/shard_map/ppermute | solution.py:364
  114.1 4.4 %collective-permute-done.20.refs_4_ = f32[4,5,4,16,128]{4,3,2,1,0:T(8,128)S(1)} collective-permute-done((f32[4,5,4,16,128]{4,3,2,1,0:T(8,128)S(1)}, f32[4,5,4,16,128]{4,3,2,1,0:T(8,128)S(1)}, u32[]{:S(2)}, u32[]{:S(2)}) %collective-permute-start.20) | collective-permute-done | bytes 655392 | tf_op jit(solution)/shard_map/ppermute | solution.py:364
  118.5 7.6 %collective-permute-done.21.refs_5_ = f32[4,5,4,16,128]{4,3,2,1,0:T(8,128)S(1)} collective-permute-done((f32[4,5,4,16,128]{4,3,2,1,0:T(8,128)S(1)}, f32[4,5,4,16,128]{4,3,2,1,0:T(8,128)S(1)}, u32[]{:S(2)}, u32[]{:S(2)}) %collective-permute-start.21) | collective-permute-done | bytes 655392 | tf_op jit(solution)/shard_map/ppermute | solution.py:364
  126.6 3.0 %collective-permute-start.24 = (f32[4,5,4,16,128]{4,3,2,1,0:T(8,128)S(1)}, f32[4,5,4,16,128]{4,3,2,1,0:T(8,128)S(1)}, u32[]{:S(2)}, u32[]{:S(2)}) collective-permute-start(f32[4,5,4,16,128]{4,3,2,1,0:T(8,128)S(1)} %get-tuple-element.37), channel_id=1, source_target_pairs={{0,48},{16,32},{32,16},{48,0},{64,112},{80,96},{96,80},{112,64},{1... | collective-permute-start | bytes 1966088 | tf_op jit(solution)/shard_map/ppermute | solution.py:364
  129.7 6.5 %collective-permute-done.28.refs_0_ = f32[4,5,4,16,128]{4,3,2,1,0:T(8,128)S(1)} collective-permute-done((f32[4,5,4,16,128]{4,3,2,1,0:T(8,128)S(1)}, f32[4,5,4,16,128]{4,3,2,1,0:T(8,128)S(1)}, u32[]{:S(2)}, u32[]{:S(2)}) %collective-permute-start.28) | collective-permute-done | bytes 655392 | tf_op jit(solution)/shard_map/ppermute | solution.py:364
  136.3 6.5 %collective-permute-done.30.refs_2_ = f32[4,5,4,16,128]{4,3,2,1,0:T(8,128)S(1)} collective-permute-done((f32[4,5,4,16,128]{4,3,2,1,0:T(8,128)S(1)}, f32[4,5,4,16,128]{4,3,2,1,0:T(8,128)S(1)}, u32[]{:S(2)}, u32[]{:S(2)}) %collective-permute-start.30) | collective-permute-done | bytes 655392 | tf_op jit(solution)/shard_map/ppermute | solution.py:364
  143.1 4.0 %shard_map.42.refs_8_ = f32[16,5,16,16,128]{4,3,2,1,0:T(8,128)} custom-call(s32[1]{0:T(128)} %bitcast.meta, f32[21,4,16,128]{3,2,1,0:T(8,128)S(1)} %copy-done.1, f32[21,4,16,128]{3,2,1,0:T(8,128)S(1)} %copy-done.3, f32[21,4,16,128]{3,2,1,0:T(8,128)S(1)} %copy-done.5, f32[21,4,16,128]{3,2,1,0:T(8,128)S(1)} %copy-done.7, ...), custom_call_target="tpu_custom_call" | custom-call | bytes 8000000 | tf_op jit(solution)/shard_map/pallas_call | solution.py:460
  147.1 1.6 %shard_map.43.refs_4_ = f32[16,5,16,16,128]{4,3,2,1,0:T(8,128)} custom-call(s32[1]{0:T(128)} %bitcast.meta, f32[4,5,4,16,128]{4,3,2,1,0:T(8,128)S(1)} %collective-permute-done.8.refs_0_, f32[4,5,4,16,128]{4,3,2,1,0:T(8,128)S(1)} %collective-permute-done.9.refs_1_, ...), custom_call_target="tpu_custom_call", output_to_operand_aliasing={{}: (9, {})} | custom-call | bytes 4000000 | tf_op jit(solution)/shard_map/pallas_call | solution.py:474
  148.8 1.6 %shard_map.44.refs_2_ = f32[16,5,16,16,128]{4,3,2,1,0:T(8,128)} custom-call(s32[1]{0:T(128)} %bitcast.meta, f32[4,5,4,16,128]{4,3,2,1,0:T(8,128)S(1)} %collective-permute-done.28.refs_0_, f32[4,5,4,16,128]{4,3,2,1,0:T(8,128)S(1)} %collective-permute-done.29.refs_1_, ...), custom_call_target="tpu_custom_call", output_to_operand_aliasing={{}: (5, {})} | custom-call | bytes 4000000 | tf_op jit(solution)/shard_map/pallas_call | solution.py:474
  151.6 1.8 %collective-permute-done.25.refs_1_ = f32[4,5,4,16,128]{4,3,2,1,0:T(8,128)S(1)} collective-permute-done((f32[4,5,4,16,128]{4,3,2,1,0:T(8,128)S(1)}, f32[4,5,4,16,128]{4,3,2,1,0:T(8,128)S(1)}, u32[]{:S(2)}, u32[]{:S(2)}) %collective-permute-start.25) | collective-permute-done | bytes 655392 | tf_op jit(solution)/shard_map/ppermute | solution.py:364
  (93 shorter events, 18.1 us)
Async XLA Ops:
  2.0 8.8 %collective-permute-start = (f32[6,2,32,128]{3,2,1,0:T(8,128)S(1)}, f32[6,2,32,128]{3,2,1,0:T(8,128)S(1)}, u32[]{:S(2)}, u32[]{:S(2)}) collective-permute-start(f32[6,2,32,128]{3,2,1,0:T(8,128)S(1)} %pad_maximum_fusion.2), channel_id=1, source_target_pairs={{0,16},{16,32},{32,48},{48,64},{64,80},{80,96},{96,112},{112,128},... | collective-permute-start | bytes 589832 | tf_op jit(solution)/shard_map/ppermute | solution.py:509
  3.9 6.9 %collective-permute-start.1 = (f32[6,2,32,128]{3,2,1,0:T(8,128)S(1)}, f32[6,2,32,128]{3,2,1,0:T(8,128)S(1)}, u32[]{:S(2)}, u32[]{:S(2)}) collective-permute-start(f32[6,2,32,128]{3,2,1,0:T(8,128)S(1)} %pad_maximum_fusion.3), channel_id=1, source_target_pairs={{0,240},{16,0},{32,16},{48,32},{64,48},{80,64},{96,80},{112,96},{1... | collective-permute-start | bytes 589832 | tf_op jit(solution)/shard_map/ppermute | solution.py:509
  11.1 8.1 %collective-permute-start.2 = (f32[6,36,2,128]{3,2,1,0:T(2,128)S(1)}, f32[6,36,2,128]{3,2,1,0:T(2,128)S(1)}, u32[]{:S(2)}, u32[]{:S(2)}) collective-permute-start(f32[6,36,2,128]{3,2,1,0:T(2,128)S(1)} %pad_maximum_fusion), channel_id=1, source_target_pairs={{0,1},{1,2},{2,3},{3,4},{4,5},{5,6},{6,7},{7,8},{8,9},{9,10},{10,1... | collective-permute-start | bytes 663560 | tf_op jit(solution)/shard_map/ppermute | solution.py:509
  11.3 7.9 %collective-permute-start.3 = (f32[6,36,2,128]{3,2,1,0:T(2,128)S(1)}, f32[6,36,2,128]{3,2,1,0:T(2,128)S(1)}, u32[]{:S(2)}, u32[]{:S(2)}) collective-permute-start(f32[6,36,2,128]{3,2,1,0:T(2,128)S(1)} %pad_maximum_fusion.1), channel_id=1, source_target_pairs={{0,15},{1,0},{2,1},{3,2},{4,3},{5,4},{6,5},{7,6},{8,7},{9,8},{10,9... | collective-permute-start | bytes 663560 | tf_op jit(solution)/shard_map/ppermute | solution.py:509
  37.5 21.0 %collective-permute-start.12 = (f32[21,4,16,128]{3,2,1,0:T(8,128)}, f32[21,4,16,128]{3,2,1,0:T(8,128)S(1)}, u32[]{:S(2)}, u32[]{:S(2)}) collective-permute-start(f32[21,4,16,128]{3,2,1,0:T(8,128)} %get-tuple-element.25.refs_0_), channel_id=1, source_target_pairs={{0,48},{16,32},{32,16},{48,0},{64,112},{80,96},{96,80},{112,64},{1... | collective-permute-start | bytes 2064392 | tf_op jit(solution)/shard_map/ppermute | solution.py:364
  42.0 16.6 %collective-permute-start.4 = (f32[21,4,16,128]{3,2,1,0:T(8,128)}, f32[21,4,16,128]{3,2,1,0:T(8,128)S(1)}, u32[]{:S(2)}, u32[]{:S(2)}) collective-permute-start(f32[21,4,16,128]{3,2,1,0:T(8,128)} %get-tuple-element.25.refs_0_), channel_id=1, source_target_pairs={{0,16},{16,0},{32,48},{48,32},{64,80},{80,64},{96,112},{112,96},{1... | collective-permute-start | bytes 2064392 | tf_op jit(solution)/shard_map/ppermute | solution.py:364
  42.0 18.0 %collective-permute-start.13 = (f32[21,4,16,128]{3,2,1,0:T(8,128)}, f32[21,4,16,128]{3,2,1,0:T(8,128)S(1)}, u32[]{:S(2)}, u32[]{:S(2)}) collective-permute-start(f32[21,4,16,128]{3,2,1,0:T(8,128)} %get-tuple-element.26.refs_1_), channel_id=1, source_target_pairs={{0,64},{16,80},{32,96},{48,112},{64,0},{80,16},{96,32},{112,48},{1... | collective-permute-start | bytes 2064392 | tf_op jit(solution)/shard_map/ppermute | solution.py:364
  42.0 29.9 %collective-permute-start.5 = (f32[21,4,16,128]{3,2,1,0:T(8,128)}, f32[21,4,16,128]{3,2,1,0:T(8,128)S(1)}, u32[]{:S(2)}, u32[]{:S(2)}) collective-permute-start(f32[21,4,16,128]{3,2,1,0:T(8,128)} %get-tuple-element.26.refs_1_), channel_id=1, source_target_pairs={{0,48},{16,32},{32,16},{48,0},{64,112},{80,96},{96,80},{112,64},{1... | collective-permute-start | bytes 2064392 | tf_op jit(solution)/shard_map/ppermute | solution.py:364
  42.3 32.5 %collective-permute-start.14 = (f32[21,4,16,128]{3,2,1,0:T(8,128)}, f32[21,4,16,128]{3,2,1,0:T(8,128)S(1)}, u32[]{:S(2)}, u32[]{:S(2)}) collective-permute-start(f32[21,4,16,128]{3,2,1,0:T(8,128)} %get-tuple-element.27.refs_2_), channel_id=1, source_target_pairs={{0,192},{16,208},{32,224},{48,240},{64,128},{80,144},{96,160},{112... | collective-permute-start | bytes 2064392 | tf_op jit(solution)/shard_map/ppermute | solution.py:364
  58.6 16.4 %collective-permute-start.6 = (f32[21,4,16,128]{3,2,1,0:T(8,128)}, f32[21,4,16,128]{3,2,1,0:T(8,128)}, u32[]{:S(2)}, u32[]{:S(2)}) collective-permute-start(f32[21,4,16,128]{3,2,1,0:T(8,128)} %get-tuple-element.27.refs_2_), channel_id=1, source_target_pairs={{0,64},{16,80},{32,96},{48,112},{64,0},{80,16},{96,32},{112,48},{1... | collective-permute-start | bytes 2064392 | tf_op jit(solution)/shard_map/ppermute | solution.py:364
  58.6 17.8 %collective-permute-start.7 = (f32[21,4,16,128]{3,2,1,0:T(8,128)}, f32[21,4,16,128]{3,2,1,0:T(8,128)}, u32[]{:S(2)}, u32[]{:S(2)}) collective-permute-start(f32[21,4,16,128]{3,2,1,0:T(8,128)} %get-tuple-element.28.refs_3_), channel_id=1, source_target_pairs={{0,192},{16,208},{32,224},{48,240},{64,128},{80,144},{96,160},{112... | collective-permute-start | bytes 2064392 | tf_op jit(solution)/shard_map/ppermute | solution.py:364
  60.0 23.8 %collective-permute-start.15 = (f32[21,4,16,128]{3,2,1,0:T(8,128)}, f32[21,4,16,128]{3,2,1,0:T(8,128)}, u32[]{:S(2)}, u32[]{:S(2)}) collective-permute-start(f32[21,4,16,128]{3,2,1,0:T(8,128)} %get-tuple-element.28.refs_3_), channel_id=1, source_target_pairs={{0,16},{16,0},{32,48},{48,32},{64,80},{80,64},{96,112},{112,96},{1... | collective-permute-start | bytes 2064392 | tf_op jit(solution)/shard_map/ppermute | solution.py:364
  71.9 17.5 %collective-permute-start.16 = (f32[21,4,16,128]{3,2,1,0:T(8,128)S(1)}, f32[21,4,16,128]{3,2,1,0:T(8,128)}, u32[]{:S(2)}, u32[]{:S(2)}) collective-permute-start(f32[21,4,16,128]{3,2,1,0:T(8,128)S(1)} %collective-permute-done.4.refs_4_), channel_id=1, source_target_pairs={{0,48},{16,32},{32,16},{48,0},{64,112},{80,96},{96,80},{112,64},{1... | collective-permute-start | bytes 2064392 | tf_op jit(solution)/shard_map/ppermute | solution.py:364
  74.9 18.5 %collective-permute-start.17 = (f32[21,4,16,128]{3,2,1,0:T(8,128)S(1)}, f32[21,4,16,128]{3,2,1,0:T(8,128)}, u32[]{:S(2)}, u32[]{:S(2)}) collective-permute-start(f32[21,4,16,128]{3,2,1,0:T(8,128)S(1)} %collective-permute-done.5.refs_5_), channel_id=1, source_target_pairs={{0,64},{16,80},{32,96},{48,112},{64,0},{80,16},{96,32},{112,48},{1... | collective-permute-start | bytes 2064392 | tf_op jit(solution)/shard_map/ppermute | solution.py:364
  75.0 18.4 %collective-permute-start.18 = (f32[21,4,16,128]{3,2,1,0:T(8,128)}, f32[21,4,16,128]{3,2,1,0:T(8,128)}, u32[]{:S(2)}, u32[]{:S(2)}) collective-permute-start(f32[21,4,16,128]{3,2,1,0:T(8,128)} %collective-permute-done.6.refs_6_), channel_id=1, source_target_pairs={{0,192},{16,208},{32,224},{48,240},{64,128},{80,144},{96,160},{112... | collective-permute-start | bytes 2064392 | tf_op jit(solution)/shard_map/ppermute | solution.py:364
  76.4 17.2 %collective-permute-start.19 = (f32[21,4,16,128]{3,2,1,0:T(8,128)}, f32[21,4,16,128]{3,2,1,0:T(8,128)}, u32[]{:S(2)}, u32[]{:S(2)}) collective-permute-start(f32[21,4,16,128]{3,2,1,0:T(8,128)} %collective-permute-done.7.refs_7_), channel_id=1, source_target_pairs={{0,16},{16,0},{32,48},{48,32},{64,80},{80,64},{96,112},{112,96},{1... | collective-permute-start | bytes 2064392 | tf_op jit(solution)/shard_map/ppermute | solution.py:364
  83.8 23.5 %collective-permute-start.8 = (f32[4,5,4,16,128]{4,3,2,1,0:T(8,128)S(1)}, f32[4,5,4,16,128]{4,3,2,1,0:T(8,128)S(1)}, u32[]{:S(2)}, u32[]{:S(2)}) collective-permute-start(f32[4,5,4,16,128]{4,3,2,1,0:T(8,128)S(1)} %get-tuple-element.29), channel_id=1, source_target_pairs={{0,64},{16,80},{32,96},{48,112},{64,0},{80,16},{96,32},{112,48},{1... | collective-permute-start | bytes 1966088 | tf_op jit(solution)/shard_map/ppermute | solution.py:364
  89.4 18.0 %collective-permute-start.9 = (f32[4,5,4,16,128]{4,3,2,1,0:T(8,128)S(1)}, f32[4,5,4,16,128]{4,3,2,1,0:T(8,128)S(1)}, u32[]{:S(2)}, u32[]{:S(2)}) collective-permute-start(f32[4,5,4,16,128]{4,3,2,1,0:T(8,128)S(1)} %get-tuple-element.30), channel_id=1, source_target_pairs={{0,192},{16,208},{32,224},{48,240},{64,128},{80,144},{96,160},{112... | collective-permute-start | bytes 1966088 | tf_op jit(solution)/shard_map/ppermute | solution.py:364
  93.3 14.0 %collective-permute-start.10 = (f32[4,5,4,16,128]{4,3,2,1,0:T(8,128)S(1)}, f32[4,5,4,16,128]{4,3,2,1,0:T(8,128)S(1)}, u32[]{:S(2)}, u32[]{:S(2)}) collective-permute-start(f32[4,5,4,16,128]{4,3,2,1,0:T(8,128)S(1)} %get-tuple-element.31), channel_id=1, source_target_pairs={{0,16},{16,0},{32,48},{48,32},{64,80},{80,64},{96,112},{112,96},{1... | collective-permute-start | bytes 1966088 | tf_op jit(solution)/shard_map/ppermute | solution.py:364
  93.3 18.2 %collective-permute-start.11 = (f32[4,5,4,16,128]{4,3,2,1,0:T(8,128)S(1)}, f32[4,5,4,16,128]{4,3,2,1,0:T(8,128)S(1)}, u32[]{:S(2)}, u32[]{:S(2)}) collective-permute-start(f32[4,5,4,16,128]{4,3,2,1,0:T(8,128)S(1)} %get-tuple-element.32), channel_id=1, source_target_pairs={{0,48},{16,32},{32,16},{48,0},{64,112},{80,96},{96,80},{112,64},{1... | collective-permute-start | bytes 1966088 | tf_op jit(solution)/shard_map/ppermute | solution.py:364
  96.0 22.5 %collective-permute-start.20 = (f32[4,5,4,16,128]{4,3,2,1,0:T(8,128)S(1)}, f32[4,5,4,16,128]{4,3,2,1,0:T(8,128)S(1)}, u32[]{:S(2)}, u32[]{:S(2)}) collective-permute-start(f32[4,5,4,16,128]{4,3,2,1,0:T(8,128)S(1)} %get-tuple-element.33), channel_id=1, source_target_pairs={{0,64},{16,80},{32,96},{48,112},{64,0},{80,16},{96,32},{112,48},{1... | collective-permute-start | bytes 1966088 | tf_op jit(solution)/shard_map/ppermute | solution.py:364
  107.3 18.9 %collective-permute-start.21 = (f32[4,5,4,16,128]{4,3,2,1,0:T(8,128)S(1)}, f32[4,5,4,16,128]{4,3,2,1,0:T(8,128)S(1)}, u32[]{:S(2)}, u32[]{:S(2)}) collective-permute-start(f32[4,5,4,16,128]{4,3,2,1,0:T(8,128)S(1)} %get-tuple-element.34), channel_id=1, source_target_pairs={{0,192},{16,208},{32,224},{48,240},{64,128},{80,144},{96,160},{112... | collective-permute-start | bytes 1966088 | tf_op jit(solution)/shard_map/ppermute | solution.py:364
  107.3 19.1 %collective-permute-start.22 = (f32[4,5,4,16,128]{4,3,2,1,0:T(8,128)S(1)}, f32[4,5,4,16,128]{4,3,2,1,0:T(8,128)S(1)}, u32[]{:S(2)}, u32[]{:S(2)}) collective-permute-start(f32[4,5,4,16,128]{4,3,2,1,0:T(8,128)S(1)} %get-tuple-element.35), channel_id=1, source_target_pairs={{0,16},{16,0},{32,48},{48,32},{64,80},{80,64},{96,112},{112,96},{1... | collective-permute-start | bytes 1966088 | tf_op jit(solution)/shard_map/ppermute | solution.py:364
  107.3 19.1 %collective-permute-start.23 = (f32[4,5,4,16,128]{4,3,2,1,0:T(8,128)S(1)}, f32[4,5,4,16,128]{4,3,2,1,0:T(8,128)S(1)}, u32[]{:S(2)}, u32[]{:S(2)}) collective-permute-start(f32[4,5,4,16,128]{4,3,2,1,0:T(8,128)S(1)} %get-tuple-element.36), channel_id=1, source_target_pairs={{0,48},{16,32},{32,16},{48,0},{64,112},{80,96},{96,80},{112,64},{1... | collective-permute-start | bytes 1966088 | tf_op jit(solution)/shard_map/ppermute | solution.py:364
  111.6 24.7 %collective-permute-start.28 = (f32[4,5,4,16,128]{4,3,2,1,0:T(8,128)S(1)}, f32[4,5,4,16,128]{4,3,2,1,0:T(8,128)S(1)}, u32[]{:S(2)}, u32[]{:S(2)}) collective-permute-start(f32[4,5,4,16,128]{4,3,2,1,0:T(8,128)S(1)} %get-tuple-element.41), channel_id=1, source_target_pairs={{0,192},{16,208},{32,224},{48,240},{64,128},{80,144},{96,160},{112... | collective-permute-start | bytes 1966088 | tf_op jit(solution)/shard_map/ppermute | solution.py:364
  118.5 17.8 %collective-permute-start.29 = (f32[4,5,4,16,128]{4,3,2,1,0:T(8,128)S(1)}, f32[4,5,4,16,128]{4,3,2,1,0:T(8,128)S(1)}, u32[]{:S(2)}, u32[]{:S(2)}) collective-permute-start(f32[4,5,4,16,128]{4,3,2,1,0:T(8,128)S(1)} %get-tuple-element.42), channel_id=1, source_target_pairs={{0,16},{16,0},{32,48},{48,32},{64,80},{80,64},{96,112},{112,96},{1... | collective-permute-start | bytes 1966088 | tf_op jit(solution)/shard_map/ppermute | solution.py:364
  126.2 16.6 %collective-permute-start.30 = (f32[4,5,4,16,128]{4,3,2,1,0:T(8,128)S(1)}, f32[4,5,4,16,128]{4,3,2,1,0:T(8,128)S(1)}, u32[]{:S(2)}, u32[]{:S(2)}) collective-permute-start(f32[4,5,4,16,128]{4,3,2,1,0:T(8,128)S(1)} %get-tuple-element.43), channel_id=1, source_target_pairs={{0,48},{16,32},{32,16},{48,0},{64,112},{80,96},{96,80},{112,64},{1... | collective-permute-start | bytes 1966088 | tf_op jit(solution)/shard_map/ppermute | solution.py:364
  126.4 22.3 %collective-permute-start.31 = (f32[4,5,4,16,128]{4,3,2,1,0:T(8,128)S(1)}, f32[4,5,4,16,128]{4,3,2,1,0:T(8,128)S(1)}, u32[]{:S(2)}, u32[]{:S(2)}) collective-permute-start(f32[4,5,4,16,128]{4,3,2,1,0:T(8,128)S(1)} %get-tuple-element.44), channel_id=1, source_target_pairs={{0,64},{16,80},{32,96},{48,112},{64,0},{80,16},{96,32},{112,48},{1... | collective-permute-start | bytes 1966088 | tf_op jit(solution)/shard_map/ppermute | solution.py:364
  126.6 24.9 %collective-permute-start.24 = (f32[4,5,4,16,128]{4,3,2,1,0:T(8,128)S(1)}, f32[4,5,4,16,128]{4,3,2,1,0:T(8,128)S(1)}, u32[]{:S(2)}, u32[]{:S(2)}) collective-permute-start(f32[4,5,4,16,128]{4,3,2,1,0:T(8,128)S(1)} %get-tuple-element.37), channel_id=1, source_target_pairs={{0,48},{16,32},{32,16},{48,0},{64,112},{80,96},{96,80},{112,64},{1... | collective-permute-start | bytes 1966088 | tf_op jit(solution)/shard_map/ppermute | solution.py:364
  136.2 14.2 %collective-permute-start.26 = (f32[4,5,4,16,128]{4,3,2,1,0:T(8,128)S(1)}, f32[4,5,4,16,128]{4,3,2,1,0:T(8,128)S(1)}, u32[]{:S(2)}, u32[]{:S(2)}) collective-permute-start(f32[4,5,4,16,128]{4,3,2,1,0:T(8,128)S(1)} %get-tuple-element.39), channel_id=1, source_target_pairs={{0,192},{16,208},{32,224},{48,240},{64,128},{80,144},{96,160},{112... | collective-permute-start | bytes 1966088 | tf_op jit(solution)/shard_map/ppermute | solution.py:364
  136.3 14.2 %collective-permute-start.27 = (f32[4,5,4,16,128]{4,3,2,1,0:T(8,128)S(1)}, f32[4,5,4,16,128]{4,3,2,1,0:T(8,128)S(1)}, u32[]{:S(2)}, u32[]{:S(2)}) collective-permute-start(f32[4,5,4,16,128]{4,3,2,1,0:T(8,128)S(1)} %get-tuple-element.40), channel_id=1, source_target_pairs={{0,16},{16,0},{32,48},{48,32},{64,80},{80,64},{96,112},{112,96},{1... | collective-permute-start | bytes 1966088 | tf_op jit(solution)/shard_map/ppermute | solution.py:364
  142.8 10.6 %collective-permute-start.25 = (f32[4,5,4,16,128]{4,3,2,1,0:T(8,128)S(1)}, f32[4,5,4,16,128]{4,3,2,1,0:T(8,128)S(1)}, u32[]{:S(2)}, u32[]{:S(2)}) collective-permute-start(f32[4,5,4,16,128]{4,3,2,1,0:T(8,128)S(1)} %get-tuple-element.38), channel_id=1, source_target_pairs={{0,64},{16,80},{32,96},{48,112},{64,0},{80,16},{96,32},{112,48},{1... | collective-permute-start | bytes 1966088 | tf_op jit(solution)/shard_map/ppermute | solution.py:364
  (12 other events, 128.7 us)

commit v2 on v1

--- a/solution.py
+++ b/solution.py
@@ -166,8 +166,8 @@
         f = [fzp[c, t] for c in range(5)]
         return [v - pltpu.roll(v, 1, 1) for v in f]
 
-    def sweep(load, x, whole):
-        cells, faces, ends, change, side = [], [], [], [], []
+    def sweep(load, x, whole, end_row):
+        cells, change, side = [], [], []
         for t in range(TILES + 1):
             u = load(x, t)
             q = prims(u)
@@ -181,8 +181,7 @@
                 for c in range(5):
                     fzp[c, t] = fz[c]
                 cells.append(u)
-                faces.append(face)
-                ends.append([face[c] + dz[c] for c in range(5)])
+                end_row(t, face, dz)
                 change.append([face[c] + walls if c == 3 else face[c] for c in range(5)])
             if 0 < t < TILES:
                 fy = rusanov(side[t - 1], side[t])
@@ -199,7 +198,7 @@
             for c in range(5):
                 d = edge[c] - outer[c]
                 change[4][c] = change[4][c] + jnp.where(top, d, -d)
-        return cells, faces, ends, change, before, after
+        return cells, change, before, after
 
     def face_slot(x):
         back = x - 2
@@ -220,13 +219,17 @@
             high.wait()
 
         slot = face_slot(x)
-        cells, faces, ends, change, before, after = sweep(load_w, x, True)
+
+        def end_row(t, face, dz):
+            for c in range(5):
+                md[c, x - 1, t] = md[c, x - 1, t] - HALF * (face[c] + dz[c])
+                if t < TILES:
+                    fxw[c, slot, t] = face[c]
+
+        cells, change, before, after = sweep(load_w, x, True, end_row)
         for c in range(5):
             for t in range(TILES + 1):
-                md[c, x - 1, t] = md[c, x - 1, t] - HALF * ends[t][c]
                 md[c, x, t] = cells[t][c] + HALF * change[t][c]
-                if t < TILES:
-                    fxw[c, slot, t] = faces[t][c]
             fyw[0, c, x] = before[c]
             fyw[1, c, x] = after[c]
         return 0
@@ -246,12 +249,17 @@
         coarse = 1.0 - fine
         fine_here = HALF * fine
         at_top, at_bottom = msk[a, 1], msk[a, 2]
-        cells, faces, ends, change, before, after = sweep(load_m, x, False)
+
+        def end_row(t, face, dz):
+            at = pl.ds(t, 8, stride=4)
+            for c in range(5):
+                fxm[c, slot, t] = face[c]
+                out[c, row, at, :] = out[c, row, at, :] - fine_back * (face[c] + dz[c])
+
+        cells, change, before, after = sweep(load_m, x, False, end_row)
         for c in range(5):
             for t in range(TILES):
-                fxm[c, slot, t] = faces[t][c]
                 at = pl.ds(t, 8, stride=4)
-                out[c, row, at, :] = out[c, row, at, :] - fine_back * ends[t][c]
                 u = cells[t][c]
                 v = u + coarse * (u - spread(wn, c, x, t)) + fine_here * change[t][c]
                 if t == 0:

time: 157 us -> 155 us (0.987)
  Pallas kernels: 34.1 us -> 32.2 us
    pallas_call x1, Pallas kernels: 17 us -> 15.2 us  [update(): pl.pallas_call(kernel, out_shape=[jax.ShapeDtypeStruct(OWN, jnp.float32)]...]
where the time goes in v2:
time: 155 us; the launch traced here: 153 us
  waiting for transfers between devices  72.7 us (47%)
  starting transfers between devices  34.4 us (22%)
  Pallas kernels  32.2 us (21%)
  local copies, waits for them, and re-layouts  12.1 us (8%)
    ppermute x28, waiting for transfers between devices, across(): lax.ppermute(block, 'gx', [(g, corner(corner(g) ^ bit(q, t))) for g in ra...  69.7 us
    ppermute x28, starting transfers between devices, across(): lax.ppermute(block, 'gx', [(g, corner(corner(g) ^ bit(q, t))) for g in ra...  25.6 us
    pallas_call x1, Pallas kernels, update(): pl.pallas_call(kernel, out_shape=[jax.ShapeDtypeStruct(OWN, jnp.float32)]...  15.2 us
    pallas_call x5, Pallas kernels, mover(): pl.pallas_call(f, out_shape=outs, in_specs=[pl.BlockSpec(memory_space=plt...  11.6 us
    ppermute x4, starting transfers between devices, shifted(): return lax.ppermute(block, axis, [(i, (i + step) % n) for i in range(n)])  8.74 us
    unnamed x24, local copies, waits for them, and re-layouts  5.72 us
    pallas_call x4, Pallas kernels, placer(): pl.pallas_call(functools.partial(place_kernel, kind, flows), out_shape=RE...  5.48 us
  transfers between devices with their start and end apart: 32, of which 13 were waited for; matrix products, arithmetic and copies ran while one was open for 3% of the time, Pallas kernels for 10%

profile of v2, /device:TPU:6, one launch (start us, length us, event | category | flops | bytes accessed | tf_op | source)
XLA Modules:
  0.0 152.8 jit_solution(12391235151243267294)
XLA Ops:
  2.0 1.7 %collective-permute-start = (f32[6,2,32,128]{3,2,1,0:T(8,128)S(1)}, f32[6,2,32,128]{3,2,1,0:T(8,128)S(1)}, u32[]{:S(2)}, u32[]{:S(2)}) collective-permute-start(f32[6,2,32,128]{3,2,1,0:T(8,128)S(1)} %pad_maximum_fusion.2), channel_id=1, source_target_pairs={{0,16},{16,32},{32,48},{48,64},{64,80},{80,96},{96,112},{112,128},... | collective-permute-start | bytes 589832 | tf_op jit(solution)/shard_map/ppermute | solution.py:517
  3.9 2.6 %collective-permute-start.1 = (f32[6,2,32,128]{3,2,1,0:T(8,128)S(1)}, f32[6,2,32,128]{3,2,1,0:T(8,128)S(1)}, u32[]{:S(2)}, u32[]{:S(2)}) collective-permute-start(f32[6,2,32,128]{3,2,1,0:T(8,128)S(1)} %pad_maximum_fusion.3), channel_id=1, source_target_pairs={{0,240},{16,0},{32,16},{48,32},{64,48},{80,64},{96,80},{112,96},{1... | collective-permute-start | bytes 589832 | tf_op jit(solution)/shard_map/ppermute | solution.py:517
  7.1 1.4 fusion
  8.6 2.2 %collective-permute-done.xlo = f32[6,2,32,128]{3,2,1,0:T(8,128)S(1)} collective-permute-done((f32[6,2,32,128]{3,2,1,0:T(8,128)S(1)}, f32[6,2,32,128]{3,2,1,0:T(8,128)S(1)}, u32[]{:S(2)}, u32[]{:S(2)}) %collective-permute-start) | collective-permute-done | bytes 196640 | tf_op jit(solution)/shard_map/ppermute | solution.py:517
  11.3 4.4 %collective-permute-start.3 = (f32[6,36,2,128]{3,2,1,0:T(2,128)S(1)}, f32[6,36,2,128]{3,2,1,0:T(2,128)S(1)}, u32[]{:S(2)}, u32[]{:S(2)}) collective-permute-start(f32[6,36,2,128]{3,2,1,0:T(2,128)S(1)} %pad_maximum_fusion.1), channel_id=1, source_target_pairs={{0,15},{1,0},{2,1},{3,2},{4,3},{5,4},{6,5},{7,6},{8,7},{9,8},{10,9... | collective-permute-start | bytes 663560 | tf_op jit(solution)/shard_map/ppermute | solution.py:517
  15.7 1.3 reshape.24.level
  17.1 1.3 reshape.25.owner
  20.5 15.2 %shard_map.37 = (f32[21,4,16,128]{3,2,1,0:T(8,128)}, f32[21,4,16,128]{3,2,1,0:T(8,128)}, f32[21,4,16,128]{3,2,1,0:T(8,128)}, f32[21,4,16,128]{3,2,1,0:T(8,128)}) custom-call(s32[4]{0:T(128)} %reshape.24.level, s32[4]{0:T(128)} %reshape.25.owner, f32[5,32,32,128]{3,2,1,0:T(8,128)} %cons.1, f32[6,2,32,128]{3,2,1,0:T(8,128)} %copy-done.8, ...), custom_call_target="tpu_custom_call" | custom-call | flops 50000000 | bytes 14000000 | tf_op jit(solution)/shard_map/pallas_call | solution.py:332
  35.7 4.5 %collective-permute-start.12 = (f32[21,4,16,128]{3,2,1,0:T(8,128)}, f32[21,4,16,128]{3,2,1,0:T(8,128)S(1)}, u32[]{:S(2)}, u32[]{:S(2)}) collective-permute-start(f32[21,4,16,128]{3,2,1,0:T(8,128)} %get-tuple-element.25.refs_0_), channel_id=1, source_target_pairs={{0,48},{16,32},{32,16},{48,0},{64,112},{80,96},{96,80},{112,64},{1... | collective-permute-start | bytes 2064392 | tf_op jit(solution)/shard_map/ppermute | solution.py:372
  40.5 1.3 collective-permute-start.14
  41.8 14.9 %collective-permute-done.12.refs_0_.refs_8_ = f32[21,4,16,128]{3,2,1,0:T(8,128)S(1)} collective-permute-done((f32[21,4,16,128]{3,2,1,0:T(8,128)}, f32[21,4,16,128]{3,2,1,0:T(8,128)S(1)}, u32[]{:S(2)}, u32[]{:S(2)}) %collective-permute-start.12) | collective-permute-done | bytes 688160 | tf_op jit(solution)/shard_map/ppermute | solution.py:372
  56.8 1.4 collective-permute-start.7
  58.2 2.6 %collective-permute-start.15 = (f32[21,4,16,128]{3,2,1,0:T(8,128)}, f32[21,4,16,128]{3,2,1,0:T(8,128)}, u32[]{:S(2)}, u32[]{:S(2)}) collective-permute-start(f32[21,4,16,128]{3,2,1,0:T(8,128)} %get-tuple-element.28.refs_3_), channel_id=1, source_target_pairs={{0,16},{16,0},{32,48},{48,32},{64,80},{80,64},{96,112},{112,96},{1... | collective-permute-start | bytes 2064392 | tf_op jit(solution)/shard_map/ppermute | solution.py:372
  60.8 9.3 %collective-permute-done.5.refs_5_ = f32[21,4,16,128]{3,2,1,0:T(8,128)S(1)} collective-permute-done((f32[21,4,16,128]{3,2,1,0:T(8,128)}, f32[21,4,16,128]{3,2,1,0:T(8,128)S(1)}, u32[]{:S(2)}, u32[]{:S(2)}) %collective-permute-start.5) | collective-permute-done | bytes 688160 | tf_op jit(solution)/shard_map/ppermute | solution.py:372
  70.1 3.0 %collective-permute-start.16 = (f32[21,4,16,128]{3,2,1,0:T(8,128)S(1)}, f32[21,4,16,128]{3,2,1,0:T(8,128)}, u32[]{:S(2)}, u32[]{:S(2)}) collective-permute-start(f32[21,4,16,128]{3,2,1,0:T(8,128)S(1)} %collective-permute-done.4.refs_4_), channel_id=1, source_target_pairs={{0,48},{16,32},{32,16},{48,0},{64,112},{80,96},{96,80},{112,64},{1... | collective-permute-start | bytes 2064392 | tf_op jit(solution)/shard_map/ppermute | solution.py:372
  73.1 1.4 collective-permute-start.18
  80.1 1.9 %shard_map.38 = (f32[4,5,4,16,128]{4,3,2,1,0:T(8,128)S(1)}, f32[4,5,4,16,128]{4,3,2,1,0:T(8,128)S(1)}, f32[4,5,4,16,128]{4,3,2,1,0:T(8,128)S(1)}, f32[4,5,4,16,128]{4,3,2,1,0:T(8,128)S(1)}) custom-call(s32[1]{0:T(128)} %bitcast.meta, f32[21,4,16,128]{3,2,1,0:T(8,128)S(1)} %copy-done, f32[21,4,16,128]{3,2,1,0:T(8,128)S(1)} %copy-done.2, ...), custom_call_target="tpu_custom_call" | custom-call | bytes 8000000 | tf_op jit(solution)/shard_map/pallas_call | solution.py:468
  82.9 4.6 %collective-permute-done.16.refs_4_.refs_12_ = f32[21,4,16,128]{3,2,1,0:T(8,128)} collective-permute-done((f32[21,4,16,128]{3,2,1,0:T(8,128)S(1)}, f32[21,4,16,128]{3,2,1,0:T(8,128)}, u32[]{:S(2)}, u32[]{:S(2)}) %collective-permute-start.16) | collective-permute-done | bytes 688160 | tf_op jit(solution)/shard_map/ppermute | solution.py:372
  87.5 4.0 %collective-permute-done.17.refs_5_.refs_13_ = f32[21,4,16,128]{3,2,1,0:T(8,128)} collective-permute-done((f32[21,4,16,128]{3,2,1,0:T(8,128)S(1)}, f32[21,4,16,128]{3,2,1,0:T(8,128)}, u32[]{:S(2)}, u32[]{:S(2)}) %collective-permute-start.17) | collective-permute-done | bytes 688160 | tf_op jit(solution)/shard_map/ppermute | solution.py:372
  91.8 2.4 %shard_map.39 = (f32[4,5,4,16,128]{4,3,2,1,0:T(8,128)S(1)}, f32[4,5,4,16,128]{4,3,2,1,0:T(8,128)S(1)}, f32[4,5,4,16,128]{4,3,2,1,0:T(8,128)S(1)}, f32[4,5,4,16,128]{4,3,2,1,0:T(8,128)S(1)}) custom-call(s32[1]{0:T(128)} %bitcast.meta, f32[21,4,16,128]{3,2,1,0:T(8,128)S(1)} %collective-permute-done.12.refs_0_.refs_8_, ...), custom_call_target="tpu_custom_call" | custom-call | bytes 8000000 | tf_op jit(solution)/shard_map/pallas_call | solution.py:468
  95.5 10.0 %collective-permute-done.8.refs_0_ = f32[4,5,4,16,128]{4,3,2,1,0:T(8,128)S(1)} collective-permute-done((f32[4,5,4,16,128]{4,3,2,1,0:T(8,128)S(1)}, f32[4,5,4,16,128]{4,3,2,1,0:T(8,128)S(1)}, u32[]{:S(2)}, u32[]{:S(2)}) %collective-permute-start.8) | collective-permute-done | bytes 655392 | tf_op jit(solution)/shard_map/ppermute | solution.py:372
  106.6 3.1 %shard_map.41 = (f32[4,5,4,16,128]{4,3,2,1,0:T(8,128)S(1)}, f32[4,5,4,16,128]{4,3,2,1,0:T(8,128)S(1)}, f32[4,5,4,16,128]{4,3,2,1,0:T(8,128)S(1)}, f32[4,5,4,16,128]{4,3,2,1,0:T(8,128)S(1)}) custom-call(s32[1]{0:T(128)} %bitcast.meta, f32[21,4,16,128]{3,2,1,0:T(8,128)S(1)} %copy-done.1, f32[21,4,16,128]{3,2,1,0:T(8,128)S(1)} %copy-done.3, ...), custom_call_target="tpu_custom_call" | custom-call | bytes 8000000 | tf_op jit(solution)/shard_map/pallas_call | solution.py:468
  109.7 2.5 %collective-permute-start.28 = (f32[4,5,4,16,128]{4,3,2,1,0:T(8,128)S(1)}, f32[4,5,4,16,128]{4,3,2,1,0:T(8,128)S(1)}, u32[]{:S(2)}, u32[]{:S(2)}) collective-permute-start(f32[4,5,4,16,128]{4,3,2,1,0:T(8,128)S(1)} %get-tuple-element.41), channel_id=1, source_target_pairs={{0,192},{16,208},{32,224},{48,240},{64,128},{80,144},{96,160},{112... | collective-permute-start | bytes 1966088 | tf_op jit(solution)/shard_map/ppermute | solution.py:372
  112.3 4.4 %collective-permute-done.20.refs_4_ = f32[4,5,4,16,128]{4,3,2,1,0:T(8,128)S(1)} collective-permute-done((f32[4,5,4,16,128]{4,3,2,1,0:T(8,128)S(1)}, f32[4,5,4,16,128]{4,3,2,1,0:T(8,128)S(1)}, u32[]{:S(2)}, u32[]{:S(2)}) %collective-permute-start.20) | collective-permute-done | bytes 655392 | tf_op jit(solution)/shard_map/ppermute | solution.py:372
  116.7 7.6 %collective-permute-done.21.refs_5_ = f32[4,5,4,16,128]{4,3,2,1,0:T(8,128)S(1)} collective-permute-done((f32[4,5,4,16,128]{4,3,2,1,0:T(8,128)S(1)}, f32[4,5,4,16,128]{4,3,2,1,0:T(8,128)S(1)}, u32[]{:S(2)}, u32[]{:S(2)}) %collective-permute-start.21) | collective-permute-done | bytes 655392 | tf_op jit(solution)/shard_map/ppermute | solution.py:372
  124.8 3.0 %collective-permute-start.24 = (f32[4,5,4,16,128]{4,3,2,1,0:T(8,128)S(1)}, f32[4,5,4,16,128]{4,3,2,1,0:T(8,128)S(1)}, u32[]{:S(2)}, u32[]{:S(2)}) collective-permute-start(f32[4,5,4,16,128]{4,3,2,1,0:T(8,128)S(1)} %get-tuple-element.37), channel_id=1, source_target_pairs={{0,48},{16,32},{32,16},{48,0},{64,112},{80,96},{96,80},{112,64},{1... | collective-permute-start | bytes 1966088 | tf_op jit(solution)/shard_map/ppermute | solution.py:372
  127.8 6.5 %collective-permute-done.28.refs_0_ = f32[4,5,4,16,128]{4,3,2,1,0:T(8,128)S(1)} collective-permute-done((f32[4,5,4,16,128]{4,3,2,1,0:T(8,128)S(1)}, f32[4,5,4,16,128]{4,3,2,1,0:T(8,128)S(1)}, u32[]{:S(2)}, u32[]{:S(2)}) %collective-permute-start.28) | collective-permute-done | bytes 655392 | tf_op jit(solution)/shard_map/ppermute | solution.py:372
  134.4 6.5 %collective-permute-done.30.refs_2_ = f32[4,5,4,16,128]{4,3,2,1,0:T(8,128)S(1)} collective-permute-done((f32[4,5,4,16,128]{4,3,2,1,0:T(8,128)S(1)}, f32[4,5,4,16,128]{4,3,2,1,0:T(8,128)S(1)}, u32[]{:S(2)}, u32[]{:S(2)}) %collective-permute-start.30) | collective-permute-done | bytes 655392 | tf_op jit(solution)/shard_map/ppermute | solution.py:372
  141.3 4.0 %shard_map.42.refs_8_ = f32[16,5,16,16,128]{4,3,2,1,0:T(8,128)} custom-call(s32[1]{0:T(128)} %bitcast.meta, f32[21,4,16,128]{3,2,1,0:T(8,128)S(1)} %copy-done.1, f32[21,4,16,128]{3,2,1,0:T(8,128)S(1)} %copy-done.3, f32[21,4,16,128]{3,2,1,0:T(8,128)S(1)} %copy-done.5, f32[21,4,16,128]{3,2,1,0:T(8,128)S(1)} %copy-done.7, ...), custom_call_target="tpu_custom_call" | custom-call | bytes 8000000 | tf_op jit(solution)/shard_map/pallas_call | solution.py:468
  145.3 1.6 %shard_map.43.refs_4_ = f32[16,5,16,16,128]{4,3,2,1,0:T(8,128)} custom-call(s32[1]{0:T(128)} %bitcast.meta, f32[4,5,4,16,128]{4,3,2,1,0:T(8,128)S(1)} %collective-permute-done.8.refs_0_, f32[4,5,4,16,128]{4,3,2,1,0:T(8,128)S(1)} %collective-permute-done.9.refs_1_, ...), custom_call_target="tpu_custom_call", output_to_operand_aliasing={{}: (9, {})} | custom-call | bytes 4000000 | tf_op jit(solution)/shard_map/pallas_call | solution.py:482
  146.9 1.6 %shard_map.44.refs_2_ = f32[16,5,16,16,128]{4,3,2,1,0:T(8,128)} custom-call(s32[1]{0:T(128)} %bitcast.meta, f32[4,5,4,16,128]{4,3,2,1,0:T(8,128)S(1)} %collective-permute-done.28.refs_0_, f32[4,5,4,16,128]{4,3,2,1,0:T(8,128)S(1)} %collective-permute-done.29.refs_1_, ...), custom_call_target="tpu_custom_call", output_to_operand_aliasing={{}: (5, {})} | custom-call | bytes 4000000 | tf_op jit(solution)/shard_map/pallas_call | solution.py:482
  149.7 1.8 %collective-permute-done.25.refs_1_ = f32[4,5,4,16,128]{4,3,2,1,0:T(8,128)S(1)} collective-permute-done((f32[4,5,4,16,128]{4,3,2,1,0:T(8,128)S(1)}, f32[4,5,4,16,128]{4,3,2,1,0:T(8,128)S(1)}, u32[]{:S(2)}, u32[]{:S(2)}) %collective-permute-start.25) | collective-permute-done | bytes 655392 | tf_op jit(solution)/shard_map/ppermute | solution.py:372
  (93 shorter events, 18.1 us)
Async XLA Ops:
  2.0 8.8 %collective-permute-start = (f32[6,2,32,128]{3,2,1,0:T(8,128)S(1)}, f32[6,2,32,128]{3,2,1,0:T(8,128)S(1)}, u32[]{:S(2)}, u32[]{:S(2)}) collective-permute-start(f32[6,2,32,128]{3,2,1,0:T(8,128)S(1)} %pad_maximum_fusion.2), channel_id=1, source_target_pairs={{0,16},{16,32},{32,48},{48,64},{64,80},{80,96},{96,112},{112,128},... | collective-permute-start | bytes 589832 | tf_op jit(solution)/shard_map/ppermute | solution.py:517
  3.9 6.9 %collective-permute-start.1 = (f32[6,2,32,128]{3,2,1,0:T(8,128)S(1)}, f32[6,2,32,128]{3,2,1,0:T(8,128)S(1)}, u32[]{:S(2)}, u32[]{:S(2)}) collective-permute-start(f32[6,2,32,128]{3,2,1,0:T(8,128)S(1)} %pad_maximum_fusion.3), channel_id=1, source_target_pairs={{0,240},{16,0},{32,16},{48,32},{64,48},{80,64},{96,80},{112,96},{1... | collective-permute-start | bytes 589832 | tf_op jit(solution)/shard_map/ppermute | solution.py:517
  11.1 8.1 %collective-permute-start.2 = (f32[6,36,2,128]{3,2,1,0:T(2,128)S(1)}, f32[6,36,2,128]{3,2,1,0:T(2,128)S(1)}, u32[]{:S(2)}, u32[]{:S(2)}) collective-permute-start(f32[6,36,2,128]{3,2,1,0:T(2,128)S(1)} %pad_maximum_fusion), channel_id=1, source_target_pairs={{0,1},{1,2},{2,3},{3,4},{4,5},{5,6},{6,7},{7,8},{8,9},{9,10},{10,1... | collective-permute-start | bytes 663560 | tf_op jit(solution)/shard_map/ppermute | solution.py:517
  11.3 7.9 %collective-permute-start.3 = (f32[6,36,2,128]{3,2,1,0:T(2,128)S(1)}, f32[6,36,2,128]{3,2,1,0:T(2,128)S(1)}, u32[]{:S(2)}, u32[]{:S(2)}) collective-permute-start(f32[6,36,2,128]{3,2,1,0:T(2,128)S(1)} %pad_maximum_fusion.1), channel_id=1, source_target_pairs={{0,15},{1,0},{2,1},{3,2},{4,3},{5,4},{6,5},{7,6},{8,7},{9,8},{10,9... | collective-permute-start | bytes 663560 | tf_op jit(solution)/shard_map/ppermute | solution.py:517
  35.7 21.0 %collective-permute-start.12 = (f32[21,4,16,128]{3,2,1,0:T(8,128)}, f32[21,4,16,128]{3,2,1,0:T(8,128)S(1)}, u32[]{:S(2)}, u32[]{:S(2)}) collective-permute-start(f32[21,4,16,128]{3,2,1,0:T(8,128)} %get-tuple-element.25.refs_0_), channel_id=1, source_target_pairs={{0,48},{16,32},{32,16},{48,0},{64,112},{80,96},{96,80},{112,64},{1... | collective-permute-start | bytes 2064392 | tf_op jit(solution)/shard_map/ppermute | solution.py:372
  40.2 16.6 %collective-permute-start.4 = (f32[21,4,16,128]{3,2,1,0:T(8,128)}, f32[21,4,16,128]{3,2,1,0:T(8,128)S(1)}, u32[]{:S(2)}, u32[]{:S(2)}) collective-permute-start(f32[21,4,16,128]{3,2,1,0:T(8,128)} %get-tuple-element.25.refs_0_), channel_id=1, source_target_pairs={{0,16},{16,0},{32,48},{48,32},{64,80},{80,64},{96,112},{112,96},{1... | collective-permute-start | bytes 2064392 | tf_op jit(solution)/shard_map/ppermute | solution.py:372
  40.2 18.0 %collective-permute-start.13 = (f32[21,4,16,128]{3,2,1,0:T(8,128)}, f32[21,4,16,128]{3,2,1,0:T(8,128)S(1)}, u32[]{:S(2)}, u32[]{:S(2)}) collective-permute-start(f32[21,4,16,128]{3,2,1,0:T(8,128)} %get-tuple-element.26.refs_1_), channel_id=1, source_target_pairs={{0,64},{16,80},{32,96},{48,112},{64,0},{80,16},{96,32},{112,48},{1... | collective-permute-start | bytes 2064392 | tf_op jit(solution)/shard_map/ppermute | solution.py:372
  40.2 29.9 %collective-permute-start.5 = (f32[21,4,16,128]{3,2,1,0:T(8,128)}, f32[21,4,16,128]{3,2,1,0:T(8,128)S(1)}, u32[]{:S(2)}, u32[]{:S(2)}) collective-permute-start(f32[21,4,16,128]{3,2,1,0:T(8,128)} %get-tuple-element.26.refs_1_), channel_id=1, source_target_pairs={{0,48},{16,32},{32,16},{48,0},{64,112},{80,96},{96,80},{112,64},{1... | collective-permute-start | bytes 2064392 | tf_op jit(solution)/shard_map/ppermute | solution.py:372
  40.5 32.5 %collective-permute-start.14 = (f32[21,4,16,128]{3,2,1,0:T(8,128)}, f32[21,4,16,128]{3,2,1,0:T(8,128)S(1)}, u32[]{:S(2)}, u32[]{:S(2)}) collective-permute-start(f32[21,4,16,128]{3,2,1,0:T(8,128)} %get-tuple-element.27.refs_2_), channel_id=1, source_target_pairs={{0,192},{16,208},{32,224},{48,240},{64,128},{80,144},{96,160},{112... | collective-permute-start | bytes 2064392 | tf_op jit(solution)/shard_map/ppermute | solution.py:372
  56.7 16.4 %collective-permute-start.6 = (f32[21,4,16,128]{3,2,1,0:T(8,128)}, f32[21,4,16,128]{3,2,1,0:T(8,128)}, u32[]{:S(2)}, u32[]{:S(2)}) collective-permute-start(f32[21,4,16,128]{3,2,1,0:T(8,128)} %get-tuple-element.27.refs_2_), channel_id=1, source_target_pairs={{0,64},{16,80},{32,96},{48,112},{64,0},{80,16},{96,32},{112,48},{1... | collective-permute-start | bytes 2064392 | tf_op jit(solution)/shard_map/ppermute | solution.py:372
  56.8 17.8 %collective-permute-start.7 = (f32[21,4,16,128]{3,2,1,0:T(8,128)}, f32[21,4,16,128]{3,2,1,0:T(8,128)}, u32[]{:S(2)}, u32[]{:S(2)}) collective-permute-start(f32[21,4,16,128]{3,2,1,0:T(8,128)} %get-tuple-element.28.refs_3_), channel_id=1, source_target_pairs={{0,192},{16,208},{32,224},{48,240},{64,128},{80,144},{96,160},{112... | collective-permute-start | bytes 2064392 | tf_op jit(solution)/shard_map/ppermute | solution.py:372
  58.2 23.8 %collective-permute-start.15 = (f32[21,4,16,128]{3,2,1,0:T(8,128)}, f32[21,4,16,128]{3,2,1,0:T(8,128)}, u32[]{:S(2)}, u32[]{:S(2)}) collective-permute-start(f32[21,4,16,128]{3,2,1,0:T(8,128)} %get-tuple-element.28.refs_3_), channel_id=1, source_target_pairs={{0,16},{16,0},{32,48},{48,32},{64,80},{80,64},{96,112},{112,96},{1... | collective-permute-start | bytes 2064392 | tf_op jit(solution)/shard_map/ppermute | solution.py:372
  70.1 17.5 %collective-permute-start.16 = (f32[21,4,16,128]{3,2,1,0:T(8,128)S(1)}, f32[21,4,16,128]{3,2,1,0:T(8,128)}, u32[]{:S(2)}, u32[]{:S(2)}) collective-permute-start(f32[21,4,16,128]{3,2,1,0:T(8,128)S(1)} %collective-permute-done.4.refs_4_), channel_id=1, source_target_pairs={{0,48},{16,32},{32,16},{48,0},{64,112},{80,96},{96,80},{112,64},{1... | collective-permute-start | bytes 2064392 | tf_op jit(solution)/shard_map/ppermute | solution.py:372
  73.0 18.5 %collective-permute-start.17 = (f32[21,4,16,128]{3,2,1,0:T(8,128)S(1)}, f32[21,4,16,128]{3,2,1,0:T(8,128)}, u32[]{:S(2)}, u32[]{:S(2)}) collective-permute-start(f32[21,4,16,128]{3,2,1,0:T(8,128)S(1)} %collective-permute-done.5.refs_5_), channel_id=1, source_target_pairs={{0,64},{16,80},{32,96},{48,112},{64,0},{80,16},{96,32},{112,48},{1... | collective-permute-start | bytes 2064392 | tf_op jit(solution)/shard_map/ppermute | solution.py:372
  73.1 18.4 %collective-permute-start.18 = (f32[21,4,16,128]{3,2,1,0:T(8,128)}, f32[21,4,16,128]{3,2,1,0:T(8,128)}, u32[]{:S(2)}, u32[]{:S(2)}) collective-permute-start(f32[21,4,16,128]{3,2,1,0:T(8,128)} %collective-permute-done.6.refs_6_), channel_id=1, source_target_pairs={{0,192},{16,208},{32,224},{48,240},{64,128},{80,144},{96,160},{112... | collective-permute-start | bytes 2064392 | tf_op jit(solution)/shard_map/ppermute | solution.py:372
  74.6 17.2 %collective-permute-start.19 = (f32[21,4,16,128]{3,2,1,0:T(8,128)}, f32[21,4,16,128]{3,2,1,0:T(8,128)}, u32[]{:S(2)}, u32[]{:S(2)}) collective-permute-start(f32[21,4,16,128]{3,2,1,0:T(8,128)} %collective-permute-done.7.refs_7_), channel_id=1, source_target_pairs={{0,16},{16,0},{32,48},{48,32},{64,80},{80,64},{96,112},{112,96},{1... | collective-permute-start | bytes 2064392 | tf_op jit(solution)/shard_map/ppermute | solution.py:372
  82.0 23.5 %collective-permute-start.8 = (f32[4,5,4,16,128]{4,3,2,1,0:T(8,128)S(1)}, f32[4,5,4,16,128]{4,3,2,1,0:T(8,128)S(1)}, u32[]{:S(2)}, u32[]{:S(2)}) collective-permute-start(f32[4,5,4,16,128]{4,3,2,1,0:T(8,128)S(1)} %get-tuple-element.29), channel_id=1, source_target_pairs={{0,64},{16,80},{32,96},{48,112},{64,0},{80,16},{96,32},{112,48},{1... | collective-permute-start | bytes 1966088 | tf_op jit(solution)/shard_map/ppermute | solution.py:372
  87.5 18.0 %collective-permute-start.9 = (f32[4,5,4,16,128]{4,3,2,1,0:T(8,128)S(1)}, f32[4,5,4,16,128]{4,3,2,1,0:T(8,128)S(1)}, u32[]{:S(2)}, u32[]{:S(2)}) collective-permute-start(f32[4,5,4,16,128]{4,3,2,1,0:T(8,128)S(1)} %get-tuple-element.30), channel_id=1, source_target_pairs={{0,192},{16,208},{32,224},{48,240},{64,128},{80,144},{96,160},{112... | collective-permute-start | bytes 1966088 | tf_op jit(solution)/shard_map/ppermute | solution.py:372
  91.5 14.0 %collective-permute-start.10 = (f32[4,5,4,16,128]{4,3,2,1,0:T(8,128)S(1)}, f32[4,5,4,16,128]{4,3,2,1,0:T(8,128)S(1)}, u32[]{:S(2)}, u32[]{:S(2)}) collective-permute-start(f32[4,5,4,16,128]{4,3,2,1,0:T(8,128)S(1)} %get-tuple-element.31), channel_id=1, source_target_pairs={{0,16},{16,0},{32,48},{48,32},{64,80},{80,64},{96,112},{112,96},{1... | collective-permute-start | bytes 1966088 | tf_op jit(solution)/shard_map/ppermute | solution.py:372
  91.5 18.2 %collective-permute-start.11 = (f32[4,5,4,16,128]{4,3,2,1,0:T(8,128)S(1)}, f32[4,5,4,16,128]{4,3,2,1,0:T(8,128)S(1)}, u32[]{:S(2)}, u32[]{:S(2)}) collective-permute-start(f32[4,5,4,16,128]{4,3,2,1,0:T(8,128)S(1)} %get-tuple-element.32), channel_id=1, source_target_pairs={{0,48},{16,32},{32,16},{48,0},{64,112},{80,96},{96,80},{112,64},{1... | collective-permute-start | bytes 1966088 | tf_op jit(solution)/shard_map/ppermute | solution.py:372
  94.2 22.5 %collective-permute-start.20 = (f32[4,5,4,16,128]{4,3,2,1,0:T(8,128)S(1)}, f32[4,5,4,16,128]{4,3,2,1,0:T(8,128)S(1)}, u32[]{:S(2)}, u32[]{:S(2)}) collective-permute-start(f32[4,5,4,16,128]{4,3,2,1,0:T(8,128)S(1)} %get-tuple-element.33), channel_id=1, source_target_pairs={{0,64},{16,80},{32,96},{48,112},{64,0},{80,16},{96,32},{112,48},{1... | collective-permute-start | bytes 1966088 | tf_op jit(solution)/shard_map/ppermute | solution.py:372
  105.4 18.9 %collective-permute-start.21 = (f32[4,5,4,16,128]{4,3,2,1,0:T(8,128)S(1)}, f32[4,5,4,16,128]{4,3,2,1,0:T(8,128)S(1)}, u32[]{:S(2)}, u32[]{:S(2)}) collective-permute-start(f32[4,5,4,16,128]{4,3,2,1,0:T(8,128)S(1)} %get-tuple-element.34), channel_id=1, source_target_pairs={{0,192},{16,208},{32,224},{48,240},{64,128},{80,144},{96,160},{112... | collective-permute-start | bytes 1966088 | tf_op jit(solution)/shard_map/ppermute | solution.py:372
  105.5 19.1 %collective-permute-start.22 = (f32[4,5,4,16,128]{4,3,2,1,0:T(8,128)S(1)}, f32[4,5,4,16,128]{4,3,2,1,0:T(8,128)S(1)}, u32[]{:S(2)}, u32[]{:S(2)}) collective-permute-start(f32[4,5,4,16,128]{4,3,2,1,0:T(8,128)S(1)} %get-tuple-element.35), channel_id=1, source_target_pairs={{0,16},{16,0},{32,48},{48,32},{64,80},{80,64},{96,112},{112,96},{1... | collective-permute-start | bytes 1966088 | tf_op jit(solution)/shard_map/ppermute | solution.py:372
  105.5 19.1 %collective-permute-start.23 = (f32[4,5,4,16,128]{4,3,2,1,0:T(8,128)S(1)}, f32[4,5,4,16,128]{4,3,2,1,0:T(8,128)S(1)}, u32[]{:S(2)}, u32[]{:S(2)}) collective-permute-start(f32[4,5,4,16,128]{4,3,2,1,0:T(8,128)S(1)} %get-tuple-element.36), channel_id=1, source_target_pairs={{0,48},{16,32},{32,16},{48,0},{64,112},{80,96},{96,80},{112,64},{1... | collective-permute-start | bytes 1966088 | tf_op jit(solution)/shard_map/ppermute | solution.py:372
  109.7 24.7 %collective-permute-start.28 = (f32[4,5,4,16,128]{4,3,2,1,0:T(8,128)S(1)}, f32[4,5,4,16,128]{4,3,2,1,0:T(8,128)S(1)}, u32[]{:S(2)}, u32[]{:S(2)}) collective-permute-start(f32[4,5,4,16,128]{4,3,2,1,0:T(8,128)S(1)} %get-tuple-element.41), channel_id=1, source_target_pairs={{0,192},{16,208},{32,224},{48,240},{64,128},{80,144},{96,160},{112... | collective-permute-start | bytes 1966088 | tf_op jit(solution)/shard_map/ppermute | solution.py:372
  116.7 17.8 %collective-permute-start.29 = (f32[4,5,4,16,128]{4,3,2,1,0:T(8,128)S(1)}, f32[4,5,4,16,128]{4,3,2,1,0:T(8,128)S(1)}, u32[]{:S(2)}, u32[]{:S(2)}) collective-permute-start(f32[4,5,4,16,128]{4,3,2,1,0:T(8,128)S(1)} %get-tuple-element.42), channel_id=1, source_target_pairs={{0,16},{16,0},{32,48},{48,32},{64,80},{80,64},{96,112},{112,96},{1... | collective-permute-start | bytes 1966088 | tf_op jit(solution)/shard_map/ppermute | solution.py:372
  124.3 16.6 %collective-permute-start.30 = (f32[4,5,4,16,128]{4,3,2,1,0:T(8,128)S(1)}, f32[4,5,4,16,128]{4,3,2,1,0:T(8,128)S(1)}, u32[]{:S(2)}, u32[]{:S(2)}) collective-permute-start(f32[4,5,4,16,128]{4,3,2,1,0:T(8,128)S(1)} %get-tuple-element.43), channel_id=1, source_target_pairs={{0,48},{16,32},{32,16},{48,0},{64,112},{80,96},{96,80},{112,64},{1... | collective-permute-start | bytes 1966088 | tf_op jit(solution)/shard_map/ppermute | solution.py:372
  124.6 22.3 %collective-permute-start.31 = (f32[4,5,4,16,128]{4,3,2,1,0:T(8,128)S(1)}, f32[4,5,4,16,128]{4,3,2,1,0:T(8,128)S(1)}, u32[]{:S(2)}, u32[]{:S(2)}) collective-permute-start(f32[4,5,4,16,128]{4,3,2,1,0:T(8,128)S(1)} %get-tuple-element.44), channel_id=1, source_target_pairs={{0,64},{16,80},{32,96},{48,112},{64,0},{80,16},{96,32},{112,48},{1... | collective-permute-start | bytes 1966088 | tf_op jit(solution)/shard_map/ppermute | solution.py:372
  124.8 24.9 %collective-permute-start.24 = (f32[4,5,4,16,128]{4,3,2,1,0:T(8,128)S(1)}, f32[4,5,4,16,128]{4,3,2,1,0:T(8,128)S(1)}, u32[]{:S(2)}, u32[]{:S(2)}) collective-permute-start(f32[4,5,4,16,128]{4,3,2,1,0:T(8,128)S(1)} %get-tuple-element.37), channel_id=1, source_target_pairs={{0,48},{16,32},{32,16},{48,0},{64,112},{80,96},{96,80},{112,64},{1... | collective-permute-start | bytes 1966088 | tf_op jit(solution)/shard_map/ppermute | solution.py:372
  134.4 14.2 %collective-permute-start.26 = (f32[4,5,4,16,128]{4,3,2,1,0:T(8,128)S(1)}, f32[4,5,4,16,128]{4,3,2,1,0:T(8,128)S(1)}, u32[]{:S(2)}, u32[]{:S(2)}) collective-permute-start(f32[4,5,4,16,128]{4,3,2,1,0:T(8,128)S(1)} %get-tuple-element.39), channel_id=1, source_target_pairs={{0,192},{16,208},{32,224},{48,240},{64,128},{80,144},{96,160},{112... | collective-permute-start | bytes 1966088 | tf_op jit(solution)/shard_map/ppermute | solution.py:372
  134.4 14.2 %collective-permute-start.27 = (f32[4,5,4,16,128]{4,3,2,1,0:T(8,128)S(1)}, f32[4,5,4,16,128]{4,3,2,1,0:T(8,128)S(1)}, u32[]{:S(2)}, u32[]{:S(2)}) collective-permute-start(f32[4,5,4,16,128]{4,3,2,1,0:T(8,128)S(1)} %get-tuple-element.40), channel_id=1, source_target_pairs={{0,16},{16,0},{32,48},{48,32},{64,80},{80,64},{96,112},{112,96},{1... | collective-permute-start | bytes 1966088 | tf_op jit(solution)/shard_map/ppermute | solution.py:372
  140.9 10.6 %collective-permute-start.25 = (f32[4,5,4,16,128]{4,3,2,1,0:T(8,128)S(1)}, f32[4,5,4,16,128]{4,3,2,1,0:T(8,128)S(1)}, u32[]{:S(2)}, u32[]{:S(2)}) collective-permute-start(f32[4,5,4,16,128]{4,3,2,1,0:T(8,128)S(1)} %get-tuple-element.38), channel_id=1, source_target_pairs={{0,64},{16,80},{32,96},{48,112},{64,0},{80,16},{96,32},{112,48},{1... | collective-permute-start | bytes 1966088 | tf_op jit(solution)/shard_map/ppermute | solution.py:372
  (12 other events, 128.7 us)
